TPU v7x, 256 devices: a whole 4x4x8 slice. The times are simulated.
256 devices in a mesh: gx: 16 (over z, core), gy: 4 (over x), gz: 4 (over y).
Axes of the slice: x: 4, y: 4, z: 8, core: 2. Of those that a mesh axis runs over, the one named last changes fastest.
Arguments:
- a_blocks: bfloat16 [64, 16, 8, 7, 4096], P('gx', 'gy', 'gz'), may hold values from -6 to 6
- prolong: bfloat16 [64, 16, 8, 4096], P('gx', 'gy', 'gz'), may hold values from -0.75 to 0.75
- pairing: int32 [32, 8, 8], P('gx', 'gy', 'gz'), may hold values 0 or 1
- route: int32 [4096, 1], P(('gx', 'gy', 'gz')), may hold values from 0 to 15; in each aligned block of 16 rows (0 to 15, 16 to 31, ...) at most 2 rows name the same one
Outputs:
- coarse_rows: bfloat16 [8192, 11, 4096], P(('gx', 'gy', 'gz'))
Inputs may be any that keep to these rules, and one draw needn't show every extreme that they name: `pairing`: 0 pairs each patch's elements along the first direction, 1 along the second. `route`: among the 16 aggregates of one device no destination is named more than 2 times, and in every draw some device names one destination exactly 2 times.
All inputs are finite; a program needn't handle non-finite values. No bound on the sum of `pairing` on one device may be relied on, other than what follows from the above.
Results may differ from a plain program's by a relative error of at most 0.0049.
Values may be sent and summed in bfloat16 or wider, within the bound.
A program may use at most 128 MiB of HBM per device.

v0:
```python
import math

import jax
import jax.numpy as jnp
from jax import lax
from jax.sharding import PartitionSpec as P

x_first_order = [0, 2, 1, 3, 4, 5, 6]
x_second_order = [0, 1, 2, 3, 4, 5, 6]
y_first_order = [0, 4, 1, 2, 3, 5, 6]
y_second_order = [0, 3, 1, 2, 4, 5, 6]


def padded_2(array, sides, width):
    for axis, dim in sides:
        devices, length = (lax.axis_size(axis), array.shape[dim])
        up = [(i, (i + 1) % devices) for i in range(devices - 1)]
        down = [(j, i) for i, j in up]
        last = lax.slice_in_dim(array, length - width, length, axis=dim)
        initial = lax.slice_in_dim(array, 0, width, axis=dim)
        before = lax.ppermute(last, axis, up)
        after = lax.ppermute(initial, axis, down)
        array = jnp.concatenate([before, array, after], axis=dim)
    return array


def neighbours(padded):
    shifted = [
        padded[1:-1, 1:-1, 1:-1],
        padded[:-2, 1:-1, 1:-1],
        padded[2:, 1:-1, 1:-1],
        padded[1:-1, :-2, 1:-1],
        padded[1:-1, 2:, 1:-1],
        padded[1:-1, 1:-1, :-2],
        padded[1:-1, 1:-1, 2:],
    ]
    return jnp.stack(shifted, axis=3)


def triple(blocks, nearby):
    block_side = math.isqrt(blocks.shape[-1])
    leading = blocks.shape[:-1]
    left_mat = blocks.reshape(leading + (block_side, block_side))
    right_mat = nearby.reshape(leading + (block_side, block_side))
    own_block = jnp.swapaxes(right_mat[..., :1, :, :], -1, -2)
    product = jnp.matmul(left_mat, right_mat, preferred_element_type=jnp.float32).astype(
        jnp.bfloat16
    )
    result = jnp.matmul(own_block, product, preferred_element_type=jnp.float32)
    return result.reshape(leading + (block_side * block_side,))


def members(element_grid, pairs):
    size_x, size_y, size_z = element_grid.shape[:3]
    trailing = element_grid.shape[3:]
    patches = element_grid.reshape((size_x // 2, 2, size_y // 2, 2, size_z) + trailing)

    def pick(upper, lower, slot_order):
        return jnp.take(patches[:, upper, :, lower], jnp.array(slot_order, dtype=jnp.int32), axis=3)

    x_one = jnp.stack([pick(0, 0, x_first_order), pick(0, 1, x_first_order)], axis=3)
    x_two = jnp.stack([pick(1, 0, x_second_order), pick(1, 1, x_second_order)], axis=3)
    y_one = jnp.stack([pick(0, 0, y_first_order), pick(1, 0, y_first_order)], axis=3)
    y_two = jnp.stack([pick(0, 1, y_second_order), pick(1, 1, y_second_order)], axis=3)
    along_x = (pairs == 0).reshape(pairs.shape + (1,) * (x_one.ndim - 3))
    member_one = jnp.where(along_x, x_one, y_one)
    member_two = jnp.where(along_x, x_two, y_two)
    return (
        member_one.reshape((-1,) + member_one.shape[4:]),
        member_two.reshape((-1,) + member_two.shape[4:]),
    )


def arrange(member_one, member_two):
    diagonal = (
        member_one[..., 0, :]
        + member_two[..., 0, :]
        + member_one[..., 1, :]
        + member_two[..., 1, :]
    )
    return jnp.concatenate(
        [diagonal[..., None, :], member_one[..., 2:, :], member_two[..., 2:, :]], axis=-2
    )


def slot_sources(routes, n_dest, capacity):
    total = routes.shape[0]
    chosen = (routes[:, None] == jnp.arange(n_dest, dtype=jnp.int32)[None, :]).astype(jnp.int32)
    before = jnp.cumsum(chosen, axis=0) - chosen
    ranking = jnp.sum(before * chosen, axis=1)
    position = routes * capacity + ranking
    targets = jnp.arange(n_dest * capacity, dtype=jnp.int32)
    matches = position[None, :] == targets[:, None]
    anchor = jnp.sum(jnp.where(matches, jnp.arange(total, dtype=jnp.int32)[None, :], 0), axis=1)
    filled = jnp.any(matches, axis=1)
    return (anchor, filled)


def pack_slots(payload, anchor, filled):
    taken = jnp.take(payload, anchor, axis=0)
    keep_row = filled.reshape(filled.shape + (1,) * (payload.ndim - 1))
    return jnp.where(keep_row, taken, jnp.zeros_like(taken))


def local(a_blocks, prolong, pairing, route):
    padded = padded_2(prolong, (("gx", 0), ("gy", 1), ("gz", 2)), 1)
    nearby = neighbours(padded)
    devices_gx = lax.axis_size("gx")
    aggregates = route.shape[0]
    capacity = max(2, 3 * aggregates // (2 * devices_gx))
    anchor, filled = slot_sources(route[:, 0], devices_gx, capacity)
    stacked = jnp.stack([a_blocks, nearby], axis=4)
    member_one, member_two = members(stacked, pairing)
    payload = jnp.stack([member_one, member_two], axis=1)
    received = lax.all_to_all(
        pack_slots(payload, anchor, filled), "gx", split_axis=0, concat_axis=0, tiled=True
    )
    galerkin = triple(received[..., 0, :], received[..., 1, :])
    return arrange(galerkin[:, 0], galerkin[:, 1]).astype(jnp.bfloat16)


def solution(mesh):
    placed = (
        P("gx", "gy", "gz", None, None),
        P("gx", "gy", "gz", None),
        P("gx", "gy", "gz"),
        P(("gx", "gy", "gz"), None),
    )
    return jax.shard_map(
        local,
        mesh=mesh,
        in_specs=placed,
        out_specs=P(("gx", "gy", "gz"), None, None),
        check_vma=False,
    )
```

profile of v0, /device:TPU:1, one launch (start us, length us, event | category | flops | bytes accessed | tf_op | source)
XLA Modules:
  0.0 424.5 jit_solution(10719393257362353818)
XLA Ops:
  0.0 1.0 fusion.19
  1.1 4.9 %collective-permute-start = (bf16[1,4,2,4096]{3,1,2,0:T(4,128)(2,1)S(1)}, bf16[1,4,2,4096]{3,1,2,0:T(4,128)(2,1)S(1)}, u32[]{:S(2)}, u32[]{:S(2)}) collective-permute-start(bf16[1,4,2,4096]{3,1,2,0:T(4,128)(2,1)S(1)} %copy.125), channel_id=1, source_target_pairs={{0,16},{16,32},{32,48},{48,64},{64,80},{80,96},{96,112},{112,128},... | collective-permute-start | bytes 196616 | tf_op jit(solution)/shard_map/ppermute | solution.py:21
  6.1 1.9 collective-permute-start.1
  8.0 0.7 fusion.13
  8.8 0.8 select_reduce_fusion.1
  9.6 0.7 multiply_add_fusion
  10.5 0.7 broadcast_compare_fusion
  11.3 0.7 pad_clamp_fusion.4
  12.0 5.4 %copy.92 = bf16[2,2,2,2,2,7,1,4096]{7,6,5,4,2,0,3,1:T(2,128)(2,1)S(1)} copy(bf16[2,2,2,2,2,7,1,4096]{7,4,5,3,2,1,0,6:T(2,128)(2,1)} %bitcast.91) | data formatting | bytes 3670016 | tf_op jit(solution)/shard_map/stack | solution.py:112
  17.4 0.5 copy_dynamic-update-slice_fusion.6
  18.3 0.4 fusion.18
  18.7 1.3 collective-permute-start.3
  20.0 4.0 collective-permute-start.2
  24.2 0.7 pad_maximum_fusion.16
  24.9 0.6 copy_dynamic-update-slice_fusion.5
  25.5 1.2 collective-permute-done.3
  26.7 1.8 collective-permute-done.2
  28.4 0.6 pad_maximum_fusion.7
  29.1 1.3 collective-permute-start.5
  30.4 4.2 collective-permute-start.4
  34.7 0.6 copy_dynamic-update-slice_fusion.4
  35.3 6.4 %collective-permute-done.5 = bf16[6,6,1,4096]{3,1,2,0:T(8,128)(2,1)S(1)} collective-permute-done((bf16[6,6,1,4096]{3,1,2,0:T(8,128)(2,1)S(1)}, bf16[6,6,1,4096]{3,1,2,0:T(8,128)(2,1)S(1)}, u32[]{:S(2)}, u32[]{:S(2)}) %collective-permute-start.5) | collective-permute-done | bytes 294944 | tf_op jit(solution)/shard_map/ppermute | solution.py:22
  41.7 0.9 collective-permute-done.4
  42.6 1.1 pad_maximum_fusion.8
  43.7 0.3 copy.84
  44.8 0.6 copy_dynamic-update-slice_fusion.3
  45.4 0.6 copy_dynamic-update-slice_fusion.2
  46.0 0.6 copy_dynamic-update-slice_fusion.1
  46.6 0.6 copy_dynamic-update-slice_fusion
  47.2 9.7 %maximum_bitcast_fusion.2 = (bf16[2,2,2,7,2,4096]{5,4,3,2,1,0:T(2,128)(2,1)}, bf16[2,2,2,7,2,4096]{5,4,3,2,1,0:T(2,128)(2,1)S(1)}, bf16[2,2,2,7,2,4096]{5,4,3,2,...) fusion(bf16[2,2,2,2,2,7,1,4096]{7,6,5,4,2,0,3,1:T(2,128)(2,1)S(1)} %copy_dynamic-update-slice_fusion, ...), kind=kLoop, calls=%fused_computation.35 | loop fusion | flops 7340032 | bytes 7340032 | tf_op jit(solution)/shard_map/squeeze | solution.py:59
  56.9 4.5 %gather_fusion.3 = bf16[7,2,2,2,2,4096]{5,4,3,2,1,0:T(2,128)(2,1)} fusion(bf16[2,2,2,7,2,4096]{5,4,3,2,1,0:T(2,128)(2,1)} %get-tuple-element.10, s32[1024]{0:T(1024)S(1)} %get-tuple-element.33), kind=kCustom, calls=%fused_computation.2.clone | custom fusion | bytes 1835036 | tf_op jit(solution)/shard_map/jit(_take)/gather | solution.py:59
  61.4 4.6 %gather_fusion.1 = bf16[7,2,2,2,2,4096]{5,4,3,2,1,0:T(2,128)(2,1)} fusion(bf16[2,2,2,7,2,4096]{5,4,3,2,1,0:T(2,128)(2,1)} %get-tuple-element.10, s32[1024]{0:T(1024)S(1)} %pad_clamp_fusion.4), kind=kCustom, calls=%fused_computation.clone | custom fusion | bytes 1835036 | tf_op jit(solution)/shard_map/jit(_take)/gather | solution.py:59
  66.0 3.3 gather_fusion.2
  69.3 3.4 gather_fusion.7
  72.7 3.4 gather_fusion.8
  76.1 3.4 gather_fusion.6
  79.5 3.5 gather_fusion.5
  83.0 2.4 gather_fusion.4
  85.4 4.1 pad_maximum_fusion.2
  89.5 2.4 copy.93
  92.0 2.6 pad_maximum_fusion.5
  94.6 2.6 copy.96
  97.2 1.6 fusion.9
  98.9 2.6 pad_maximum_fusion.4
  101.5 2.4 copy.95
  103.9 2.6 pad_maximum_fusion.3
  106.5 2.4 copy.94
  109.0 4.7 %broadcast_select_fusion.3 = (bf16[16,1,7,2,4096]{4,3,2,0,1:T(2,128)(2,1)S(1)}, bf16[16,1,7,2,4096]{4,3,2,0,1:T(2,128)(2,1)S(1)}) fusion(bf16[16,1,7,2,4096]{4,3,2,0,1:T(2,128)(2,1)S(1)} %bitcast.80, bf16[16,1,7,2,4096]{4,3,2,0,1:T(2,128)(2,1)S(1)} %bitcast.83, pred[16]{0:T(512)(128)(4,1)S(1)} %broadcast_in_dim.67, ...), kind=kLoop, calls=%fused_computation.20 | loop fusion | flops 1835008 | bytes 11010064 | tf_op jit(solution)/shard_map/jit(_where)/select_n | solution.py:66
  113.6 7.3 %pad_maximum_fusion = bf16[16,2,7,2,4096]{4,3,2,0,1:T(2,128)(2,1)} fusion(bf16[16,1,7,2,4096]{4,3,2,0,1:T(2,128)(2,1)S(1)} %get-tuple-element.27, bf16[16,1,7,2,4096]{4,3,2,0,1:T(2,128)(2,1)S(1)} %get-tuple-element.26), kind=kLoop, calls=%fused_computation.16 | loop fusion | flops 1835008 | bytes 7340032 | tf_op jit(solution)/shard_map/stack | solution.py:114
  120.9 18.4 %gather_fusion = bf16[32,2,7,2,4096]{4,3,2,1,0:T(2,128)(2,1)} fusion(bf16[16,2,7,2,4096]{4,3,2,0,1:T(2,128)(2,1)} %pad_maximum_fusion, s32[1024]{0:T(1024)S(1)} %get-tuple-element.30), kind=kCustom, calls=%fused_computation.8 | custom fusion | bytes 14680192 | tf_op jit(solution)/shard_map/jit(_take)/gather | solution.py:100
  139.3 10.3 %broadcast_select_fusion.1 = bf16[32,2,7,2,4096]{4,3,2,1,0:T(2,128)(2,1)S(1)} fusion(pred[32]{0:T(512)(128)(4,1)S(1)} %fusion.12, bf16[32,2,7,2,4096]{4,3,2,1,0:T(2,128)(2,1)} %gather_fusion, pred[32]{0:T(512)(128)(4,1)S(1)} %compare_and_fusion), kind=kLoop, calls=%fused_computation.10 | loop fusion | flops 7340032 | bytes 14680128 | tf_op jit(solution)/shard_map/jit(_where)/select_n | solution.py:102
  149.6 171.8 %all_to_all.5 = bf16[32,2,7,2,4096]{4,3,2,1,0:T(2,128)(2,1)} all-to-all(bf16[32,2,7,2,4096]{4,3,2,1,0:T(2,128)(2,1)S(1)} %broadcast_select_fusion.1), channel_id=1, replica_groups=mesh['gx'=16,'gy'=4,'gz'=4] {'gx'}, dimensions={0} | all-to-all | bytes 14680064 | tf_op jit(solution)/shard_map/all_to_all | solution.py:115
  321.4 33.7 %fusion.16 = (bf16[32,2,7,1,4096]{4,3,2,1,0:T(2,128)(2,1)}, bf16[32,2,7,4096]{3,2,1,0:T(8,128)(2,1)}) fusion(bf16[32,2,7,2,4096]{4,3,2,1,0:T(2,128)(2,1)} %all_to_all.5), kind=kLoop, calls=%fused_computation.82 | loop fusion | bytes 14680064 | tf_op jit(solution)/shard_map/slice | solution.py:118
  355.1 9.1 %copy.97 = bf16[32,2,7,1,4096]{4,0,2,1,3:T(8,128)(2,1)} copy(bf16[32,2,7,1,4096]{4,3,2,1,0:T(2,128)(2,1)} %get-tuple-element.8) | data formatting | bytes 7340032 | tf_op jit(solution)/shard_map/slice | solution.py:118
  364.2 11.0 %reshape_squeeze.6 = bf16[32,2,7,64,64]{4,3,0,2,1:T(8,128)(2,1)} reshape(bf16[32,2,7,1,4096]{4,0,2,1,3:T(8,128)(2,1)} %copy.97) | data formatting | bytes 7340032 | tf_op jit(solution)/shard_map/reshape;squeeze | solution.py:44
  375.3 1.3 slice.151
  376.6 0.7 copy.106
  377.2 11.8 %reshape.185 = bf16[32,2,7,64,64]{4,3,2,1,0:T(8,128)(2,1)} reshape(bf16[32,2,7,4096]{3,2,1,0:T(8,128)(2,1)} %get-tuple-element.9) | data formatting | bytes 7340032 | tf_op jit(solution)/shard_map/reshape;squeeze | solution.py:43
  389.0 10.6 %convolution_bitcast_fusion = f32[32,2,7,64,64]{4,3,2,1,0:T(8,128)} fusion(bf16[32,2,7,64,64]{4,3,2,1,0:T(8,128)(2,1)} %reshape.185, bf16[32,2,7,64,64]{4,3,0,2,1:T(8,128)(2,1)} %reshape_squeeze.6, bf16[32,2,1,64,64]{3,4,1,0,2:T(8,128)(2,1)S(1)} %copy.106), kind=kOutput, calls=%fused_computation.11 | convolution fusion | flops 471597056 | bytes 15204352 | tf_op jit(solution)/shard_map/dot_general | solution.py:49
  399.6 14.1 %reshape.186 = f32[32,2,7,4096]{3,2,1,0:T(8,128)} reshape(f32[32,2,7,64,64]{4,3,2,1,0:T(8,128)} %convolution_bitcast_fusion) | data formatting | bytes 14680064 | tf_op jit(solution)/shard_map/reshape | solution.py:50
  413.7 4.0 fusion.15
  417.7 2.1 copy.128
  420.0 2.1 copy.127
  422.4 1.9 pad_maximum_fusion.1
  (45 shorter events, 2.3 us)
Async XLA Ops:
  0.0 18.0 %copy-start.8 = (s32[7]{0:T(128)S(1)}, s32[7]{0:T(128)}, u32[]{:S(2)}) copy-start(s32[7]{0:T(128)} %constant.109) | copy-start | bytes 88
  0.0 18.0 %copy-start.7 = (s32[7]{0:T(128)S(1)}, s32[7]{0:T(128)}, u32[]{:S(2)}) copy-start(s32[7]{0:T(128)} %constant.111) | copy-start | bytes 88
  0.0 17.4 %copy-start.6 = (bf16[4,4,2,4096]{3,2,1,0:T(2,128)(2,1)S(1)}, bf16[4,4,2,4096]{3,2,1,0:T(2,128)(2,1)}, u32[]{:S(2)}) copy-start(bf16[4,4,2,4096]{3,2,1,0:T(2,128)(2,1)} %param.15) | copy-start | bytes 786436
  1.1 16.9 %collective-permute-start = (bf16[1,4,2,4096]{3,1,2,0:T(4,128)(2,1)S(1)}, bf16[1,4,2,4096]{3,1,2,0:T(4,128)(2,1)S(1)}, u32[]{:S(2)}, u32[]{:S(2)}) collective-permute-start(bf16[1,4,2,4096]{3,1,2,0:T(4,128)(2,1)S(1)} %copy.125), channel_id=1, source_target_pairs={{0,16},{16,32},{32,48},{48,64},{64,80},{80,96},{96,112},{112,128},... | collective-permute-start | bytes 196616 | tf_op jit(solution)/shard_map/ppermute | solution.py:21
  6.1 12.2 %collective-permute-start.1 = (bf16[1,4,2,4096]{3,1,2,0:T(4,128)(2,1)S(1)}, bf16[1,4,2,4096]{3,1,2,0:T(4,128)(2,1)S(1)}, u32[]{:S(2)}, u32[]{:S(2)}) collective-permute-start(bf16[1,4,2,4096]{3,1,2,0:T(4,128)(2,1)S(1)} %copy.126), channel_id=1, source_target_pairs={{16,0},{32,16},{48,32},{64,48},{80,64},{96,80},{112,96},{128,112},... | collective-permute-start | bytes 196616 | tf_op jit(solution)/shard_map/ppermute | solution.py:22
  18.7 7.9 %collective-permute-start.3 = (bf16[6,1,2,4096]{3,1,2,0:T(2,128)(2,1)S(1)}, bf16[6,1,2,4096]{3,1,2,0:T(2,128)(2,1)S(1)}, u32[]{:S(2)}, u32[]{:S(2)}) collective-permute-start(bf16[6,1,2,4096]{3,1,2,0:T(2,128)(2,1)S(1)} %get-tuple-element.20), channel_id=1, source_target_pairs={{4,0},{8,4},{12,8},{5,1},{9,5},{13,9},{6,2},{10,6},{14,10},{7,3},{... | collective-permute-start | bytes 294920 | tf_op jit(solution)/shard_map/ppermute | solution.py:22
  20.0 8.4 %collective-permute-start.2 = (bf16[6,1,2,4096]{3,1,2,0:T(2,128)(2,1)S(1)}, bf16[6,1,2,4096]{3,1,2,0:T(2,128)(2,1)S(1)}, u32[]{:S(2)}, u32[]{:S(2)}) collective-permute-start(bf16[6,1,2,4096]{3,1,2,0:T(2,128)(2,1)S(1)} %get-tuple-element.21), channel_id=1, source_target_pairs={{0,4},{4,8},{8,12},{1,5},{5,9},{9,13},{2,6},{6,10},{10,14},{3,7},{... | collective-permute-start | bytes 294920 | tf_op jit(solution)/shard_map/ppermute | solution.py:21
  29.1 12.6 %collective-permute-start.5 = (bf16[6,6,1,4096]{3,1,2,0:T(8,128)(2,1)S(1)}, bf16[6,6,1,4096]{3,1,2,0:T(8,128)(2,1)S(1)}, u32[]{:S(2)}, u32[]{:S(2)}) collective-permute-start(bf16[6,6,1,4096]{3,1,2,0:T(8,128)(2,1)S(1)} %get-tuple-element.16), channel_id=1, source_target_pairs={{1,0},{2,1},{3,2},{5,4},{6,5},{7,6},{9,8},{10,9},{11,10},{13,12},{... | collective-permute-start | bytes 884744 | tf_op jit(solution)/shard_map/ppermute | solution.py:22
  30.4 12.1 %collective-permute-start.4 = (bf16[6,6,1,4096]{3,1,2,0:T(8,128)(2,1)S(1)}, bf16[6,6,1,4096]{3,1,2,0:T(8,128)(2,1)S(1)}, u32[]{:S(2)}, u32[]{:S(2)}) collective-permute-start(bf16[6,6,1,4096]{3,1,2,0:T(8,128)(2,1)S(1)} %get-tuple-element.17), channel_id=1, source_target_pairs={{0,1},{1,2},{2,3},{4,5},{5,6},{6,7},{8,9},{9,10},{10,11},{12,13},{... | collective-permute-start | bytes 884744 | tf_op jit(solution)/shard_map/ppermute | solution.py:21
  72.7 12.7 %copy-start.2 = (bf16[7,2,2,2,2,4096]{5,4,3,2,1,0:T(2,128)(2,1)S(1)}, bf16[7,2,2,2,2,4096]{5,4,3,2,1,0:T(2,128)(2,1)}, u32[]{:S(2)}) copy-start(bf16[7,2,2,2,2,4096]{5,4,3,2,1,0:T(2,128)(2,1)} %gather_fusion.1) | copy-start | bytes 2752516
  85.4 6.5 %copy-start.1 = (bf16[7,2,2,2,2,4096]{5,4,3,2,1,0:T(2,128)(2,1)S(1)}, bf16[7,2,2,2,2,4096]{5,4,3,2,1,0:T(2,128)(2,1)}, u32[]{:S(2)}) copy-start(bf16[7,2,2,2,2,4096]{5,4,3,2,1,0:T(2,128)(2,1)} %gather_fusion.7) | copy-start | bytes 2752516
  85.4 6.5 %copy-start.3 = (bf16[7,2,2,2,2,4096]{5,4,3,2,1,0:T(2,128)(2,1)S(1)}, bf16[7,2,2,2,2,4096]{5,4,3,2,1,0:T(2,128)(2,1)}, u32[]{:S(2)}) copy-start(bf16[7,2,2,2,2,4096]{5,4,3,2,1,0:T(2,128)(2,1)} %gather_fusion.8) | copy-start | bytes 2752516
  91.9 5.3 %copy-start.4 = (bf16[7,2,2,2,2,4096]{5,4,3,2,1,0:T(2,128)(2,1)S(1)}, bf16[7,2,2,2,2,4096]{5,4,3,2,1,0:T(2,128)(2,1)}, u32[]{:S(2)}) copy-start(bf16[7,2,2,2,2,4096]{5,4,3,2,1,0:T(2,128)(2,1)} %gather_fusion.6) | copy-start | bytes 2752516
  92.0 5.3 %copy-start.5 = (bf16[7,2,2,2,2,4096]{5,4,3,2,1,0:T(2,128)(2,1)S(1)}, bf16[7,2,2,2,2,4096]{5,4,3,2,1,0:T(2,128)(2,1)}, u32[]{:S(2)}) copy-start(bf16[7,2,2,2,2,4096]{5,4,3,2,1,0:T(2,128)(2,1)} %gather_fusion.5) | copy-start | bytes 2752516
  98.9 5.1 %copy-start = (bf16[7,2,2,2,2,4096]{5,4,3,2,1,0:T(2,128)(2,1)S(1)}, bf16[7,2,2,2,2,4096]{5,4,3,2,1,0:T(2,128)(2,1)}, u32[]{:S(2)}) copy-start(bf16[7,2,2,2,2,4096]{5,4,3,2,1,0:T(2,128)(2,1)} %gather_fusion.3) | copy-start | bytes 2752516
where the time goes:
time: 433 us; the launch traced here: 424 us
  blocking collectives  172 us (40%)
  local copies, waits for them, and re-layouts  160 us (37%)
  other arithmetic  53.6 us (12%)
  starting transfers between devices  17.7 us (4%)
  matrix products  10.6 us (2%)
  waiting for transfers between devices  10.2 us (2%)
    all_to_all x1, blocking collectives, local(): lax.all_to_all(pack_slots(payload, anchor, filled), 'gx', split_axis=0, c...  172 us
    slice x2, local copies, waits for them, and re-layouts, local(): galerkin = triple(received[..., 0, :], received[..., 1, :])  42.9 us
    gather x8, local copies, waits for them, and re-layouts, pick(): jnp.take(patches[:, upper, :, lower], jnp.array(slot_order, dtype=jnp.int...  28.5 us
    gather x1, local copies, waits for them, and re-layouts, pack_slots(): taken = jnp.take(payload, anchor, axis=0)  18.4 us
    reshape x1, local copies, waits for them, and re-layouts, triple(): return result.reshape(leading + (block_side * block_side,))  14.1 us
    ppermute x3, starting transfers between devices, padded_2(): before = lax.ppermute(last, axis, up)  13.2 us
    another operation x1, local copies, waits for them, and re-layouts, triple(): left_mat = blocks.reshape(leading + (block_side, block_side))  11.8 us
    another operation x1, local copies, waits for them, and re-layouts, triple(): right_mat = nearby.reshape(leading + (block_side, block_side))  11 us
  transfers between devices with their start and end apart: 6, of which 4 were waited for; matrix products, arithmetic and copies ran while one was open for 3% of the time, Pallas kernels for 0%

commit v1 on v0

--- a/solution.py
+++ b/solution.py
@@ -109,14 +109,12 @@
     aggregates = route.shape[0]
     capacity = max(2, 3 * aggregates // (2 * devices_gx))
     anchor, filled = slot_sources(route[:, 0], devices_gx, capacity)
-    stacked = jnp.stack([a_blocks, nearby], axis=4)
-    member_one, member_two = members(stacked, pairing)
-    payload = jnp.stack([member_one, member_two], axis=1)
-    received = lax.all_to_all(
-        pack_slots(payload, anchor, filled), "gx", split_axis=0, concat_axis=0, tiled=True
+    galerkin = triple(a_blocks, nearby)
+    member_one, member_two = members(galerkin, pairing)
+    coarse = arrange(member_one, member_two).astype(jnp.bfloat16)
+    return lax.all_to_all(
+        pack_slots(coarse, anchor, filled), "gx", split_axis=0, concat_axis=0, tiled=True
     )
-    galerkin = triple(received[..., 0, :], received[..., 1, :])
-    return arrange(galerkin[:, 0], galerkin[:, 1]).astype(jnp.bfloat16)
 
 
 def solution(mesh):

time: 433 us -> 242 us (0.56)
  local copies, waits for them, and re-layouts: 160 us -> 74.5 us
  blocking collectives: 172 us -> 104 us
  other arithmetic: 53.6 us -> 22.6 us
    all_to_all x1, blocking collectives: 172 us -> 104 us  [local(): lax.all_to_all(pack_slots(coarse, anchor, filled), 'gx', split_axis=0, co...]
    slice x8 -> x0, local copies, waits for them, and re-layouts: 49.2 us -> none  [the longest x2 42.9 us: local(): galerkin = triple(received[..., 0, :], received[..., 1, :])]
    another operation x4 -> x2, local copies, waits for them, and re-layouts: 28.2 us -> 7.76 us  [the longest x1 7.76 us: members(): element_grid.reshape((size_x // 2, 2, size_y // 2, 2, size_z) + trailing)]
    gather x1, local copies, waits for them, and re-layouts: 18.4 us -> 2.88 us  [pack_slots(): taken = jnp.take(payload, anchor, axis=0)]
    reshape x1, local copies, waits for them, and re-layouts: 14.1 us -> 3.71 us  [triple(): left_mat = blocks.reshape(leading + (block_side, block_side))]
    squeeze x1 -> x0, other arithmetic: 9.67 us -> none  [pick(): patches[:, upper, :, lower]]
    gather x8, local copies, waits for them, and re-layouts: 28.5 us -> 20.1 us  [pick(): jnp.take(patches[:, upper, :, lower], jnp.array(slot_order, dtype=jnp.int...]
    transpose x0 -> x1, local copies, waits for them, and re-layouts: none -> 7.9 us  [triple(): result = jnp.matmul(own_block, product, preferred_element_type=jnp.float32)]
  transfers between devices with their start and end apart: 6 -> 6, of which waited for: 4 -> 3; matrix products, arithmetic and copies ran while one was open for 3% -> 8% of each run, Pallas kernels for 0% -> 0%
where the time goes in v1:
time: 242 us; the launch traced here: 238 us
  blocking collectives  104 us (43%)
  local copies, waits for them, and re-layouts  74.5 us (31%)
  other arithmetic  22.6 us (9%)
  starting transfers between devices  16.2 us (7%)
  waiting for transfers between devices  10.2 us (4%)
  matrix products  9.1 us (4%)
    all_to_all x1, blocking collectives, local(): lax.all_to_all(pack_slots(coarse, anchor, filled), 'gx', split_axis=0, co...  104 us
    gather x8, local copies, waits for them, and re-layouts, pick(): jnp.take(patches[:, upper, :, lower], jnp.array(slot_order, dtype=jnp.int...  20.1 us
    ppermute x3, starting transfers between devices, padded_2(): before = lax.ppermute(last, axis, up)  11.1 us
    dot_general x1, matrix products, triple(): result = jnp.matmul(own_block, product, preferred_element_type=jnp.float32)  9.1 us
    unnamed x44, local copies, waits for them, and re-layouts  8.39 us
    transpose x1, local copies, waits for them, and re-layouts, triple(): result = jnp.matmul(own_block, product, preferred_element_type=jnp.float32)  7.9 us
    another operation x1, local copies, waits for them, and re-layouts, members(): element_grid.reshape((size_x // 2, 2, size_y // 2, 2, size_z) + trailing)  7.76 us
    ppermute x3, waiting for transfers between devices, padded_2(): after = lax.ppermute(initial, axis, down)  6.87 us
  transfers between devices with their start and end apart: 6, of which 3 were waited for; matrix products, arithmetic and copies ran while one was open for 8% of the time, Pallas kernels for 0%

profile of v1, /device:TPU:1, one launch (start us, length us, event | category | flops | bytes accessed | tf_op | source)
XLA Modules:
  0.0 237.7 jit_solution(1519547141941547573)
XLA Ops:
  0.0 1.1 fusion.21
  1.2 4.9 %collective-permute-start = (bf16[1,4,2,4096]{3,1,2,0:T(4,128)(2,1)S(1)}, bf16[1,4,2,4096]{3,1,2,0:T(4,128)(2,1)}, u32[]{:S(2)}, u32[]{:S(2)}) collective-permute-start(bf16[1,4,2,4096]{3,1,2,0:T(4,128)(2,1)S(1)} %copy.155), channel_id=1, source_target_pairs={{0,16},{16,32},{32,48},{48,64},{64,80},{80,96},{96,112},{112,128},... | collective-permute-start | bytes 196616 | tf_op jit(solution)/shard_map/ppermute | solution.py:21
  6.1 0.7 copy.156
  6.8 2.1 collective-permute-start.1
  8.9 1.3 stack.68
  10.2 0.7 fusion.17
  11.0 0.8 select_reduce_fusion.1
  11.8 0.7 multiply_add_fusion
  13.1 0.6 fusion.16
  14.0 1.0 constant_dynamic-update-slice_fusion.9
  15.0 3.7 %reshape.61 = bf16[4,4,2,7,64,64]{5,4,2,3,1,0:T(8,128)(2,1)} reshape(bf16[4,4,2,7,4096]{4,2,3,1,0:T(2,128)(2,1)S(1)} %copy-done.5) | data formatting | bytes 3670016 | tf_op jit(solution)/shard_map/reshape | solution.py:43
  18.8 0.7 broadcast_in_dim.67
  19.5 0.6 pad_clamp_fusion
  20.1 0.9 constant_dynamic-update-slice_fusion.2
  21.2 0.9 constant_dynamic-update-slice_fusion
  22.5 2.9 %collective-permute-start.2 = (bf16[6,1,2,4096]{3,1,2,0:T(2,128)(2,1)S(1)}, bf16[6,1,2,4096]{3,1,2,0:T(2,128)(2,1)S(1)}, u32[]{:S(2)}, u32[]{:S(2)}) collective-permute-start(bf16[6,1,2,4096]{3,1,2,0:T(2,128)(2,1)S(1)} %get-tuple-element.17), channel_id=1, source_target_pairs={{0,4},{4,8},{8,12},{1,5},{5,9},{9,13},{2,6},{6,10},{10,14},{3,7},{... | collective-permute-start | bytes 294920 | tf_op jit(solution)/shard_map/ppermute | solution.py:21
  25.4 1.3 collective-permute-start.3
  26.7 0.5 broadcast_compare_fusion.1
  27.2 0.9 copy.92
  28.1 0.9 copy.94
  29.1 3.9 %collective-permute-done.3 = bf16[6,1,2,4096]{3,1,2,0:T(2,128)(2,1)S(1)} collective-permute-done((bf16[6,1,2,4096]{3,1,2,0:T(2,128)(2,1)S(1)}, bf16[6,1,2,4096]{3,1,2,0:T(2,128)(2,1)S(1)}, u32[]{:S(2)}, u32[]{:S(2)}) %collective-permute-start.3) | collective-permute-done | bytes 98336 | tf_op jit(solution)/shard_map/ppermute | solution.py:22
  33.0 0.6 pad_maximum_fusion.5
  33.6 0.8 fusion.19
  34.4 3.2 %collective-permute-start.4 = (bf16[6,6,1,4096]{3,1,2,0:T(8,128)(2,1)}, bf16[6,6,1,4096]{3,1,2,0:T(8,128)(2,1)S(1)}, u32[]{:S(2)}, u32[]{:S(2)}) collective-permute-start(bf16[6,6,1,4096]{3,1,2,0:T(8,128)(2,1)} %get-tuple-element.13), channel_id=1, source_target_pairs={{0,1},{1,2},{2,3},{4,5},{5,6},{6,7},{8,9},{9,10},{10,11},{12,13},{... | collective-permute-start | bytes 884744 | tf_op jit(solution)/shard_map/ppermute | solution.py:21
  37.6 1.8 collective-permute-start.5
  39.4 0.7 pad_maximum_fusion.14
  41.4 1.0 constant_dynamic-update-slice_fusion.8
  42.4 0.9 constant_dynamic-update-slice_fusion.7
  43.4 3.3 %collective-permute-done.4 = bf16[6,6,1,4096]{3,1,2,0:T(8,128)(2,1)S(1)} collective-permute-done((bf16[6,6,1,4096]{3,1,2,0:T(8,128)(2,1)}, bf16[6,6,1,4096]{3,1,2,0:T(8,128)(2,1)S(1)}, u32[]{:S(2)}, u32[]{:S(2)}) %collective-permute-start.4) | collective-permute-done | bytes 294944 | tf_op jit(solution)/shard_map/ppermute | solution.py:21
  46.7 0.7 copy-done.8
  47.4 3.0 %collective-permute-done.5 = bf16[6,6,1,4096]{3,1,2,0:T(8,128)(2,1)} collective-permute-done((bf16[6,6,1,4096]{3,1,2,0:T(8,128)(2,1)S(1)}, bf16[6,6,1,4096]{3,1,2,0:T(8,128)(2,1)}, u32[]{:S(2)}, u32[]{:S(2)}) %collective-permute-start.5) | collective-permute-done | bytes 294944 | tf_op jit(solution)/shard_map/ppermute | solution.py:22
  50.4 2.4 pad_maximum_fusion.6
  55.7 0.9 constant_dynamic-update-slice_fusion.6
  56.6 0.9 constant_dynamic-update-slice_fusion.5
  57.6 1.0 constant_dynamic-update-slice_fusion.4
  58.5 1.0 constant_dynamic-update-slice_fusion.3
  59.5 9.1 %fusion.9 = f32[4,4,2,7,64,64]{4,5,3,2,1,0:T(8,128)} fusion(bf16[4,4,2,7,64,64]{4,5,3,2,1,0:T(8,128)(2,1)} %constant_dynamic-update-slice_fusion.3, bf16[4,4,2,7,64,64]{5,4,2,3,1,0:T(8,128)(2,1)} %reshape.61, bf16[4,4,2,1,64,64]{5,4,2,1,0,3:T(8,128)(2,1)S(1)} %stack.68), kind=kOutput, calls=%fused_computation.15 | convolution fusion | flops 235798528 | bytes 7602176 | tf_op jit(solution)/shard_map/dot_general | solution.py:49
  68.6 7.9 %copy.109 = f32[4,4,2,7,64,64]{5,4,2,3,1,0:T(8,128)} copy(f32[4,4,2,7,64,64]{4,5,3,2,1,0:T(8,128)} %fusion.9) | data formatting | bytes 7340032 | tf_op jit(solution)/shard_map/transpose | solution.py:49
  76.5 7.8 %reshape_reshape.3 = f32[2,2,2,2,2,7,4096]{6,4,5,3,2,1,0:T(2,128)} reshape(f32[4,4,2,7,64,64]{5,4,2,3,1,0:T(8,128)} %copy.109) | data formatting | bytes 7340032 | tf_op jit(solution)/shard_map/reshape;reshape | solution.py:56
  84.3 3.3 %slice_bitcast_fusion.3 = (f32[2,2,2,7,4096]{4,2,3,1,0:T(2,128)S(1)}, f32[2,2,2,7,4096]{4,2,3,1,0:T(2,128)S(1)}, f32[2,2,2,7,4096]{4,2,3,1,0:T(2,128)S(1)}, f32[2,2,2,7,4096]{4,2,3,1,0:T(2,128)}) fusion(f32[2,2,2,2,2,7,4096]{6,4,5,3,2,1,0:T(2,128)} %reshape_reshape.3), kind=kLoop, calls=%fused_computation.28 | loop fusion | bytes 7340032 | tf_op jit(solution)/shard_map/squeeze | solution.py:59
  87.6 2.4 %gather_fusion.5 = f32[7,2,2,2,4096]{4,3,2,1,0:T(2,128)} fusion(f32[2,2,2,7,4096]{4,2,3,1,0:T(2,128)S(1)} %get-tuple-element.7, s32[1024]{0:T(1024)S(1)} %get-tuple-element.28), kind=kCustom, calls=%fused_computation.4.clone | custom fusion | bytes 1835036 | tf_op jit(solution)/shard_map/jit(_take)/gather | solution.py:59
  90.0 3.6 %gather_fusion.6 = f32[7,2,2,2,4096]{4,3,2,1,0:T(2,128)} fusion(f32[2,2,2,7,4096]{4,2,3,1,0:T(2,128)} %get-tuple-element.9, s32[1024]{0:T(1024)S(1)} %get-tuple-element.28), kind=kCustom, calls=%fused_computation.5.clone | custom fusion | bytes 1835036 | tf_op jit(solution)/shard_map/jit(_take)/gather | solution.py:59
  93.6 3.7 %gather_fusion.8 = f32[7,2,2,2,4096]{4,3,2,1,0:T(2,128)} fusion(f32[2,2,2,7,4096]{4,2,3,1,0:T(2,128)} %get-tuple-element.9, s32[1024]{0:T(1024)S(1)} %get-tuple-element.27), kind=kCustom, calls=%fused_computation.7.clone | custom fusion | bytes 1835036 | tf_op jit(solution)/shard_map/jit(_take)/gather | solution.py:59
  97.3 2.5 %gather_fusion.7 = f32[7,2,2,2,4096]{4,3,2,1,0:T(2,128)} fusion(f32[2,2,2,7,4096]{4,2,3,1,0:T(2,128)S(1)} %get-tuple-element.8, s32[1024]{0:T(1024)S(1)} %get-tuple-element.27), kind=kCustom, calls=%fused_computation.6.clone | custom fusion | bytes 1835036 | tf_op jit(solution)/shard_map/jit(_take)/gather | solution.py:59
  99.8 2.4 %gather_fusion.2 = f32[7,2,2,2,4096]{4,3,2,1,0:T(2,128)} fusion(f32[2,2,2,7,4096]{4,2,3,1,0:T(2,128)S(1)} %get-tuple-element.8, s32[1024]{0:T(1024)S(1)} %pad_clamp_fusion.4), kind=kCustom, calls=%fused_computation.1.clone | custom fusion | bytes 1835036 | tf_op jit(solution)/shard_map/jit(_take)/gather | solution.py:59
  102.2 2.4 %gather_fusion.1 = f32[7,2,2,2,4096]{4,3,2,1,0:T(2,128)} fusion(f32[2,2,2,7,4096]{4,2,3,1,0:T(2,128)S(1)} %get-tuple-element.6, s32[1024]{0:T(1024)S(1)} %pad_clamp_fusion.4), kind=kCustom, calls=%fused_computation.clone | custom fusion | bytes 1835036 | tf_op jit(solution)/shard_map/jit(_take)/gather | solution.py:59
  104.7 1.5 gather_fusion.3
  106.2 1.5 gather_fusion.4
  107.7 2.5 %select_bitcast_fusion.1 = (f32[2,2,2,1,7,4096]{5,2,1,0,4,3:T(2,128)S(1)}, f32[2,2,2,1,7,4096]{5,2,1,0,4,3:T(2,128)S(1)}) fusion(f32[7,2,2,2,4096]{4,3,2,1,0:T(2,128)} %gather_fusion.5, pred[7]{0:T(512)(128)(4,1)S(1)} %copy-done.16, f32[7,2,2,2,4096]{4,3,2,1,0:T(2,128)} %gather_fusion.6), kind=kLoop, calls=%fused_computation.30 | loop fusion | flops 458752 | bytes 3670023 | tf_op jit(solution)/shard_map/stack | solution.py:62
  110.3 1.7 pad_maximum_fusion.3
  111.9 1.1 copy.136
  113.0 1.9 pad_maximum_fusion.4
  114.9 1.1 copy.137
  116.0 1.7 pad_maximum_fusion.1
  117.6 1.1 copy.134
  118.7 1.0 pad_maximum_fusion.2
  119.7 1.1 copy.135
  120.8 1.1 bitcast_select_fusion.1
  122.1 0.6 fusion.15
  122.9 1.2 pad_maximum_fusion
  124.2 2.9 %gather_fusion = bf16[32,11,4096]{2,1,0:T(8,128)(2,1)} fusion(bf16[16,11,4096]{2,1,0:T(8,128)(2,1)S(1)} %pad_maximum_fusion, s32[1024]{0:T(1024)} %get-tuple-element.26), kind=kCustom, calls=%fused_computation.8 | custom fusion | bytes 5767296 | tf_op jit(solution)/shard_map/jit(_take)/gather | solution.py:100
  127.1 2.7 %select_select_fusion = bf16[32,11,4096]{2,1,0:T(8,128)(2,1)S(1)} fusion(bf16[32,11,4096]{2,1,0:T(8,128)(2,1)} %gather_fusion, pred[32]{0:T(512)(128)(4,1)S(1)} %copy-done.11, pred[32]{0:T(512)(128)(4,1)S(1)} %copy-done.12), kind=kLoop, calls=%fused_computation.9 | loop fusion | flops 2883584 | bytes 5767232 | tf_op jit(solution)/shard_map/jit(_where)/select_n | solution.py:102
  129.8 104.4 %all_to_all.5 = bf16[32,11,4096]{2,1,0:T(8,128)(2,1)S(1)} all-to-all(bf16[32,11,4096]{2,1,0:T(8,128)(2,1)S(1)} %select_select_fusion), channel_id=1, replica_groups=mesh['gx'=16,'gy'=4,'gz'=4] {'gx'}, dimensions={0} | all-to-all | bytes 5767168 | tf_op jit(solution)/shard_map/all_to_all | solution.py:115
  234.2 3.3 %copy.122 = bf16[32,11,4096]{2,0,1:T(8,128)(2,1)} copy(bf16[32,11,4096]{2,1,0:T(8,128)(2,1)S(1)} %all_to_all.5) | data formatting | bytes 5767168 | tf_op jit(solution)/shard_map/all_to_all | solution.py:115
  (63 shorter events, 6.3 us)
Async XLA Ops:
  0.0 15.0 %copy-start.5 = (bf16[4,4,2,7,4096]{4,2,3,1,0:T(2,128)(2,1)S(1)}, bf16[4,4,2,7,4096]{4,2,3,1,0:T(2,128)(2,1)}, u32[]{:S(2)}) copy-start(bf16[4,4,2,7,4096]{4,2,3,1,0:T(2,128)(2,1)} %param.14) | copy-start | bytes 5505028
  1.2 18.9 %collective-permute-start = (bf16[1,4,2,4096]{3,1,2,0:T(4,128)(2,1)S(1)}, bf16[1,4,2,4096]{3,1,2,0:T(4,128)(2,1)}, u32[]{:S(2)}, u32[]{:S(2)}) collective-permute-start(bf16[1,4,2,4096]{3,1,2,0:T(4,128)(2,1)S(1)} %copy.155), channel_id=1, source_target_pairs={{0,16},{16,32},{32,48},{48,64},{64,80},{80,96},{96,112},{112,128},... | collective-permute-start | bytes 196616 | tf_op jit(solution)/shard_map/ppermute | solution.py:21
  6.8 14.4 %collective-permute-start.1 = (bf16[1,4,2,4096]{3,1,2,0:T(4,128)(2,1)}, bf16[1,4,2,4096]{3,1,2,0:T(4,128)(2,1)}, u32[]{:S(2)}, u32[]{:S(2)}) collective-permute-start(bf16[1,4,2,4096]{3,1,2,0:T(4,128)(2,1)} %copy.156), channel_id=1, source_target_pairs={{16,0},{32,16},{48,32},{64,48},{80,64},{96,80},{112,96},{128,112},... | collective-permute-start | bytes 196616 | tf_op jit(solution)/shard_map/ppermute | solution.py:22
  13.7 5.0 %copy-start.10 = (s32[2,2,2]{2,1,0:T(2,128)S(1)}, s32[2,2,2]{2,1,0:T(2,128)}, u32[]{:S(2)}) copy-start(s32[2,2,2]{2,1,0:T(2,128)} %param.16) | copy-start | bytes 100
  13.7 5.7 %copy-start.15 = (s32[7]{0:T(128)S(1)}, s32[7]{0:T(128)}, u32[]{:S(2)}) copy-start(s32[7]{0:T(128)} %constant.109) | copy-start | bytes 88
  13.7 5.7 %copy-start.14 = (s32[7]{0:T(128)S(1)}, s32[7]{0:T(128)}, u32[]{:S(2)}) copy-start(s32[7]{0:T(128)} %constant.111) | copy-start | bytes 88
  13.7 6.3 %copy-start.13 = (s32[7]{0:T(128)S(1)}, s32[7]{0:T(128)}, u32[]{:S(2)}) copy-start(s32[7]{0:T(128)} %constant.107) | copy-start | bytes 88
  13.7 7.2 %copy-start.4 = (bf16[4,4,2,4096]{3,2,1,0:T(2,128)(2,1)S(1)}, bf16[4,4,2,4096]{3,2,1,0:T(2,128)(2,1)}, u32[]{:S(2)}) copy-start(bf16[4,4,2,4096]{3,2,1,0:T(2,128)(2,1)} %param.15) | copy-start | bytes 786436
  22.5 6.6 %collective-permute-start.2 = (bf16[6,1,2,4096]{3,1,2,0:T(2,128)(2,1)S(1)}, bf16[6,1,2,4096]{3,1,2,0:T(2,128)(2,1)S(1)}, u32[]{:S(2)}, u32[]{:S(2)}) collective-permute-start(bf16[6,1,2,4096]{3,1,2,0:T(2,128)(2,1)S(1)} %get-tuple-element.17), channel_id=1, source_target_pairs={{0,4},{4,8},{8,12},{1,5},{5,9},{9,13},{2,6},{6,10},{10,14},{3,7},{... | collective-permute-start | bytes 294920 | tf_op jit(solution)/shard_map/ppermute | solution.py:21
  25.4 7.5 %collective-permute-start.3 = (bf16[6,1,2,4096]{3,1,2,0:T(2,128)(2,1)S(1)}, bf16[6,1,2,4096]{3,1,2,0:T(2,128)(2,1)S(1)}, u32[]{:S(2)}, u32[]{:S(2)}) collective-permute-start(bf16[6,1,2,4096]{3,1,2,0:T(2,128)(2,1)S(1)} %get-tuple-element.16), channel_id=1, source_target_pairs={{4,0},{8,4},{12,8},{5,1},{9,5},{13,9},{6,2},{10,6},{14,10},{7,3},{... | collective-permute-start | bytes 294920 | tf_op jit(solution)/shard_map/ppermute | solution.py:22
  29.1 11.1 %copy-start.6 = (bf16[6,1,2,4096]{3,1,2,0:T(2,128)(2,1)}, bf16[6,1,2,4096]{3,1,2,0:T(2,128)(2,1)S(1)}, u32[]{:S(2)}) copy-start(bf16[6,1,2,4096]{3,1,2,0:T(2,128)(2,1)S(1)} %collective-permute-done.2) | copy-start | bytes 294916
  33.0 7.2 %copy-start.7 = (bf16[6,1,2,4096]{3,1,2,0:T(2,128)(2,1)}, bf16[6,1,2,4096]{3,1,2,0:T(2,128)(2,1)S(1)}, u32[]{:S(2)}) copy-start(bf16[6,1,2,4096]{3,1,2,0:T(2,128)(2,1)S(1)} %collective-permute-done.3) | copy-start | bytes 294916
  34.4 12.2 %collective-permute-start.4 = (bf16[6,6,1,4096]{3,1,2,0:T(8,128)(2,1)}, bf16[6,6,1,4096]{3,1,2,0:T(8,128)(2,1)S(1)}, u32[]{:S(2)}, u32[]{:S(2)}) collective-permute-start(bf16[6,6,1,4096]{3,1,2,0:T(8,128)(2,1)} %get-tuple-element.13), channel_id=1, source_target_pairs={{0,1},{1,2},{2,3},{4,5},{5,6},{6,7},{8,9},{9,10},{10,11},{12,13},{... | collective-permute-start | bytes 884744 | tf_op jit(solution)/shard_map/ppermute | solution.py:21
  37.6 12.8 %collective-permute-start.5 = (bf16[6,6,1,4096]{3,1,2,0:T(8,128)(2,1)S(1)}, bf16[6,6,1,4096]{3,1,2,0:T(8,128)(2,1)}, u32[]{:S(2)}, u32[]{:S(2)}) collective-permute-start(bf16[6,6,1,4096]{3,1,2,0:T(8,128)(2,1)S(1)} %get-tuple-element.12), channel_id=1, source_target_pairs={{1,0},{2,1},{3,2},{5,4},{6,5},{7,6},{9,8},{10,9},{11,10},{13,12},{... | collective-permute-start | bytes 884744 | tf_op jit(solution)/shard_map/ppermute | solution.py:22
  46.7 0.7 copy-start.8
  102.2 5.5 %copy-start.16 = (pred[7]{0:T(512)(128)(4,1)S(1)}, pred[7]{0:T(512)(128)(4,1)}, u32[]{:S(2)}) copy-start(pred[7]{0:T(512)(128)(4,1)} %broadcast_compare_fusion.1) | copy-start | bytes 25
  110.2 2.8 %copy-start.1 = (f32[7,2,2,2,4096]{4,3,2,1,0:T(2,128)S(1)}, f32[7,2,2,2,4096]{4,3,2,1,0:T(2,128)}, u32[]{:S(2)}) copy-start(f32[7,2,2,2,4096]{4,3,2,1,0:T(2,128)} %gather_fusion.8) | copy-start | bytes 2752516
  110.2 2.8 %copy-start.2 = (f32[7,2,2,2,4096]{4,3,2,1,0:T(2,128)S(1)}, f32[7,2,2,2,4096]{4,3,2,1,0:T(2,128)}, u32[]{:S(2)}) copy-start(f32[7,2,2,2,4096]{4,3,2,1,0:T(2,128)} %gather_fusion.7) | copy-start | bytes 2752516
  113.0 3.0 %copy-start = (f32[7,2,2,2,4096]{4,3,2,1,0:T(2,128)S(1)}, f32[7,2,2,2,4096]{4,3,2,1,0:T(2,128)}, u32[]{:S(2)}) copy-start(f32[7,2,2,2,4096]{4,3,2,1,0:T(2,128)} %gather_fusion.2) | copy-start | bytes 2752516
  113.0 3.0 %copy-start.3 = (f32[7,2,2,2,4096]{4,3,2,1,0:T(2,128)S(1)}, f32[7,2,2,2,4096]{4,3,2,1,0:T(2,128)}, u32[]{:S(2)}) copy-start(f32[7,2,2,2,4096]{4,3,2,1,0:T(2,128)} %gather_fusion.1) | copy-start | bytes 2752516
  118.7 2.0 copy-start.9
  124.2 2.9 %copy-start.11 = (pred[32]{0:T(512)(128)(4,1)S(1)}, pred[32]{0:T(512)(128)(4,1)}, u32[]{:S(2)}) copy-start(pred[32]{0:T(512)(128)(4,1)} %compare_and_fusion) | copy-start | bytes 100
  124.2 2.9 %copy-start.12 = (pred[32]{0:T(512)(128)(4,1)S(1)}, pred[32]{0:T(512)(128)(4,1)}, u32[]{:S(2)}) copy-start(pred[32]{0:T(512)(128)(4,1)} %fusion.16) | copy-start | bytes 100

commit v2 on v1

v2 whole, which is shorter than its diff:
```python
import jax
import jax.numpy as jnp
from jax import lax
from jax.experimental import pallas as pl
from jax.experimental.pallas import tpu as pltpu
from jax.sharding import PartitionSpec as P

MESH = pl.DeviceIdType.MESH
F32 = jnp.float32
BF16 = jnp.bfloat16
GX, GY, GZ = 16, 4, 4


def iota(shape, dim):
    return lax.broadcasted_iota(jnp.int32, shape, dim)


def ones_where(cond):
    return jnp.where(cond, 1.0, 0.0).astype(BF16)


def dot(a, b):
    return jnp.dot(a, b, preferred_element_type=F32)


def kernel(pair_ref, route_ref, a_ref, p_ref, out_ref,
           nn, nr, ppt, hx, hy, hz, zs, gal, rows, send, recv, anchors,
           hs_sem, hr_sem, s_sem, r_sem):
    gx, gy, gz = lax.axis_index("gx"), lax.axis_index("gy"), lax.axis_index("gz")

    barrier = pltpu.get_barrier_semaphore()

    def greet(k, carry):
        pl.semaphore_signal(barrier, inc=1, device_id={"gx": lax.rem(gx + k, GX)}, device_id_type=MESH)
        return carry

    lax.fori_loop(1, GX, greet, 0)
    sides = (
        (gx > 0, {"gx": gx - 1}), (gx < GX - 1, {"gx": gx + 1}),
        (gy > 0, {"gy": gy - 1}), (gy < GY - 1, {"gy": gy + 1}),
        (gz > 0, {"gz": gz - 1}), (gz < GZ - 1, {"gz": gz + 1}),
    )
    for there, device in sides[2:]:
        @pl.when(there)
        def _():
            pl.semaphore_signal(barrier, inc=1, device_id=device, device_id_type=MESH)

    left = iota((64, 128), 1) < 64

    ci, ki = iota((64, 128), 0), iota((64, 128), 1)
    order = ones_where(((ki // 2) % 32 == ci // 2) & (ki // 64 == (ci + ki) % 2))
    ri, li = iota((128, 128), 0), iota((128, 128), 1)
    spread = ones_where(li % 64 == 2 * (ri % 32) + (ri // 32) % 2)
    same_z = li % 2 == ri // 64
    z_lane = (ri % 2) == (li // 64)
    half_row = (ri // 64) == (li // 64)

    def prepare(i, carry):
        for u in range(2):
            xy = 2 * i + u
            raw = p_ref[xy].astype(F32)
            both = jnp.concatenate([raw, pltpu.roll(raw, 64, 1)], axis=0)
            tile = dot(order, jnp.where(z_lane, both, 0.0).astype(BF16))
            nn[xy // 4, xy % 4] = tile.astype(BF16)
            turned = pltpu.roll(tile, 64, 1)
            nr[xy] = turned.astype(BF16)
            twice = jnp.concatenate([raw, raw], axis=0)
            twice = jnp.where(half_row, twice, 0.0).astype(BF16)
            t = lax.dot_general(spread, twice, (((1,), (1,)), ((), ())), preferred_element_type=F32)
            ppt[xy] = jnp.where(same_z, t, 0.0).astype(BF16)
            if u == 0:
                low, high = tile, turned
            else:
                zs[0, i] = jnp.where(left, low, turned).astype(BF16)
                zs[1, i] = jnp.where(left, high, tile).astype(BF16)
        return carry

    lax.fori_loop(0, 8, prepare, 0)

    near = jnp.int32(GX - 1)
    for there, _ in sides[2:]:
        near = near + there.astype(jnp.int32)
    pl.semaphore_wait(barrier, near)

    faces = (
        (nn.at[0], hx.at[1]), (nn.at[3], hx.at[0]),
        (nn.at[:, 0], hy.at[1]), (nn.at[:, 3], hy.at[0]),
        (zs.at[0], hz.at[1]), (zs.at[1], hz.at[0]),
    )
    own_halo = (hx.at[0], hx.at[1], hy.at[0], hy.at[1], hz.at[0], hz.at[1])

    def halo(i):
        source, target = faces[i]
        return pltpu.make_async_remote_copy(
            src_ref=source, dst_ref=target, send_sem=hs_sem.at[i], recv_sem=hr_sem.at[i],
            device_id=sides[i][1], device_id_type=MESH,
        )

    for i in range(6):
        @pl.when(sides[i][0])
        def _():
            halo(i).start()

        @pl.when(jnp.logical_not(sides[i][0]))
        def _():
            own_halo[i][...] = jnp.zeros(own_halo[i].shape, BF16)

    zero = jnp.zeros((64, 128), BF16)
    left32 = iota((32, 128), 1) < 64

    def product(xy, s, near_tile):
        wide = jnp.concatenate(
            [jnp.concatenate([near_tile, zero], axis=1), jnp.concatenate([zero, near_tile], axis=1)], axis=0
        )
        mixed = dot(a_ref[xy, s], wide).astype(BF16)
        mixed = jnp.concatenate([mixed[:, :128], mixed[:, 128:]], axis=0)
        g = dot(ppt[xy], mixed)
        gal[xy * 14 + 2 * s] = jnp.where(left32, g[0:32], pltpu.roll(g[32:64], 64, 1))
        gal[xy * 14 + 2 * s + 1] = jnp.where(left32, pltpu.roll(g[64:96], 64, 1), g[96:128])

    def loop(n, body):
        def step(i, carry):
            body(i)
            return carry
        lax.fori_loop(0, n, step, 0)

    @pl.loop(0, 4)
    def _(x):
        for y in range(4):
            product(x * 4 + y, 0, nn[x, y])

    @pl.loop(0, 3)
    def _(i):
        for k in range(4):
            product(i * 4 + 4 + k, 1, nn[i, k])
            product(i * 4 + k, 2, nn[i + 1, k])

    @pl.loop(0, 3)
    def _(i):
        for k in range(4):
            product(k * 4 + i + 1, 3, nn[k, i])
            product(k * 4 + i, 4, nn[k, i + 1])

    for i in range(6):
        @pl.when(sides[i][0])
        def _():
            j = i ^ 1
            source, target = faces[j]
            pltpu.make_async_remote_copy(
                src_ref=source, dst_ref=target, send_sem=hs_sem.at[j], recv_sem=hr_sem.at[j],
                device_id=sides[i][1], device_id_type=MESH,
            ).wait_recv()

    @pl.loop(0, 4)
    def _(k):
        product(k, 1, hx[0, k])
        product(12 + k, 2, hx[1, k])
        product(k * 4, 3, hy[0, k])
        product(k * 4 + 3, 4, hy[1, k])

    @pl.loop(0, 8)
    def _(q):
        below, above = hz[0, q].astype(F32), hz[1, q].astype(F32)
        below = (below, pltpu.roll(below, 64, 1))
        above = (pltpu.roll(above, 64, 1), above)
        for u in range(2):
            xy = 2 * q + u
            own = nr[xy]
            product(xy, 5, jnp.where(left, below[u].astype(BF16), own))
            product(xy, 6, jnp.where(left, own, above[u].astype(BF16)))

    @pl.loop(0, GX)
    def _(d):
        def look(k, state):
            one, two = state
            hit = route_ref[k] == d
            two = jnp.where(hit & (one < 16) & (two == 16), k, two)
            one = jnp.where(hit & (one == 16), k, one)
            return one, two

        one, two = lax.fori_loop(0, 16, look, (jnp.int32(16), jnp.int32(16)))
        anchors[2 * d] = one
        anchors[2 * d + 1] = two

    @pl.loop(0, 16)
    def _(k):
        a, b, z, t = k // 8, (k // 4) % 2, (k // 2) % 2, k % 2
        along = pair_ref[k // 2] == 0
        corner = a * 8 + b * 2
        first = jnp.where(along, corner + t, corner + 4 * t)
        second = jnp.where(along, corner + 4 + t, corner + 4 * t + 1)

        def block(xy, s):
            return gal[xy * 14 + 2 * s + z]

        rows[k, 0] = (
            block(first, 0) + block(second, 0)
            + block(first, jnp.where(along, 2, 4)) + block(second, jnp.where(along, 1, 3))
        ).astype(BF16)
        slots_x = ((1, 3, 4, 5, 6), (2, 3, 4, 5, 6))
        slots_y = ((1, 2, 3, 5, 6), (1, 2, 4, 5, 6))
        for i, xy in enumerate((first, second)):
            for j in range(5):
                rows[k, 1 + 5 * i + j] = block(xy, jnp.where(along, slots_x[i][j], slots_y[i][j])).astype(BF16)

    def pick(d, c):
        k = anchors[2 * d + c]
        row = rows[jnp.minimum(k, 15)]
        return jnp.where(k < 16, row, jnp.zeros_like(row))

    def outgoing(k):
        return pltpu.make_async_remote_copy(
            src_ref=send.at[k], dst_ref=recv.at[gx], send_sem=s_sem.at[k], recv_sem=r_sem.at[k],
            device_id={"gx": lax.rem(gx + k, GX)}, device_id_type=MESH,
        )

    @pl.loop(1, GX)
    def _(k):
        d = lax.rem(gx + k, GX)
        for c in range(2):
            send[k, c] = pick(d, c)
        outgoing(k).start()

    for c in range(2):
        recv[gx, c] = pick(gx, c)

    for i in range(6):
        @pl.when(sides[i][0])
        def _():
            halo(i).wait_send()

    pi, qi = iota((256, 256), 0), iota((256, 256), 1)
    turn = ones_where((qi % 32 == pi // 8) & (qi // 32 == pi % 8))

    for g in range(2):
        @pl.loop(8 * g, 8 * g + 8)
        def _(s):
            k = lax.rem(gx - s + GX, GX)

            @pl.when(k != 0)
            def _():
                pltpu.make_async_remote_copy(
                    src_ref=send.at[k], dst_ref=recv.at[s], send_sem=s_sem.at[k], recv_sem=r_sem.at[k],
                    device_id={"gx": s}, device_id_type=MESH,
                ).wait_recv()

        @pl.loop(0, 11)
        def _(b):
            parts = []
            for h in range(2):
                x = jnp.concatenate(
                    [recv[8 * g + 4 * h + s, c, b] for s in range(4) for c in range(2)], axis=0
                )
                parts.append(dot(turn, x).reshape(32, 8, 128))
            tile = jnp.concatenate(parts, axis=1).astype(BF16)
            for j in range(32):
                out_ref[b, pl.ds(16 * g, 16), pl.ds(128 * j, 128)] = tile[j]

    @pl.loop(1, GX)
    def _(k):
        outgoing(k).wait_send()


def local(a_blocks, prolong, pairing, route):
    a = a_blocks.reshape(4, 4, 2, 7, 32, 128).transpose(0, 1, 3, 4, 2, 5).reshape(16, 7, 64, 128)
    p = prolong.reshape(4, 4, 2, 32, 128).transpose(0, 1, 3, 2, 4).reshape(16, 64, 128)
    smem = pl.BlockSpec(memory_space=pltpu.SMEM)
    vmem = pl.BlockSpec(memory_space=pltpu.VMEM)
    out = pl.pallas_call(
        kernel,
        out_shape=jax.ShapeDtypeStruct((11, 32, 4096), BF16),
        in_specs=[smem, smem, vmem, vmem],
        out_specs=vmem,
        scratch_shapes=[
            pltpu.VMEM((4, 4, 64, 128), BF16),
            pltpu.VMEM((16, 64, 128), BF16),
            pltpu.VMEM((16, 128, 128), BF16),
            pltpu.VMEM((2, 4, 64, 128), BF16),
            pltpu.VMEM((2, 4, 64, 128), BF16),
            pltpu.VMEM((2, 8, 64, 128), BF16),
            pltpu.VMEM((2, 8, 64, 128), BF16),
            pltpu.VMEM((224, 32, 128), F32),
            pltpu.VMEM((16, 11, 32, 128), BF16),
            pltpu.VMEM((16, 2, 11, 32, 128), BF16),
            pltpu.VMEM((16, 2, 11, 32, 128), BF16),
            pltpu.SMEM((32,), jnp.int32),
            pltpu.SemaphoreType.DMA((6,)),
            pltpu.SemaphoreType.DMA((6,)),
            pltpu.SemaphoreType.DMA((16,)),
            pltpu.SemaphoreType.DMA((16,)),
        ],
        compiler_params=pltpu.CompilerParams(
            collective_id=0, has_side_effects=True, vmem_limit_bytes=48 << 20
        ),
        cost_estimate=pl.CostEstimate(flops=1 << 30, bytes_accessed=8 << 20, transcendentals=0),
    )(pairing.reshape(8), route.reshape(16), a, p)
    return out.transpose(1, 0, 2)


def solution(mesh):
    placed = (
        P("gx", "gy", "gz", None, None),
        P("gx", "gy", "gz", None),
        P("gx", "gy", "gz"),
        P(("gx", "gy", "gz"), None),
    )
    return jax.shard_map(
        local,
        mesh=mesh,
        in_specs=placed,
        out_specs=P(("gx", "gy", "gz"), None, None),
        check_vma=False,
    )
```

time: 242 us -> 98.1 us (0.41); the launches traced: 238 us -> 97.9 us
  blocking collectives: 104 us -> 0 us
  Pallas kernels: 0 us -> 92.5 us
  local copies, waits for them, and re-layouts: 74.5 us -> 5.45 us
  other arithmetic: 22.6 us -> 0 us
  starting transfers between devices: 16.2 us -> 0 us
  waiting for transfers between devices: 10.2 us -> 0 us
  matrix products: 9.1 us -> 0 us
    all_to_all x1 -> x0, blocking collectives: 104 us -> none  [local(): lax.all_to_all(pack_slots(coarse, anchor, filled), 'gx', split_axis=0, co...]
    pallas_call x0 -> x1, Pallas kernels: none -> 92.5 us  [local(): pl.pallas_call(kernel, out_shape=jax.ShapeDtypeStruct((11, 32, 4096), BF1...]
    gather x9 -> x0, local copies, waits for them, and re-layouts: 23 us -> none  [the longest x8 20.1 us: pick(): jnp.take(patches[:, upper, :, lower], jnp.array(slot_order, dtype=jnp.int...]
    another operation x21 -> x0, local copies, waits for them, and re-layouts: 18.7 us -> none  [the longest x1 7.76 us: members(): element_grid.reshape((size_x // 2, 2, size_y // 2, 2, size_z) + trailing)]
    ppermute x6 -> x0, starting transfers between devices: 16.2 us -> none  [the longest x3 11.1 us: padded_2(): before = lax.ppermute(last, axis, up)]
    ppermute x6 -> x0, waiting for transfers between devices: 10.2 us -> none  [the longest x3 6.87 us: padded_2(): after = lax.ppermute(initial, axis, down)]
    another operation x7 -> x0, other arithmetic: 9.22 us -> none  [the longest x2 4.15 us: members(): jnp.stack([pick(1, 0, x_second_order), pick(1, 1, x_second_order)], axis=3)]
    dot_general x1 -> x0, matrix products: 9.1 us -> none  [triple(): result = jnp.matmul(own_block, product, preferred_element_type=jnp.float32)]
  transfers between devices with their start and end apart: 6 -> 0, of which waited for: 3 -> 0; matrix products, arithmetic and copies ran while one was open for 8% -> 0% of each run, Pallas kernels for 0% -> 0%
where the time goes in v2:
time: 98.1 us; the launch traced here: 97.9 us
  Pallas kernels  92.5 us (94%)
  local copies, waits for them, and re-layouts  5.45 us (6%)
    pallas_call x1, Pallas kernels, local(): pl.pallas_call(kernel, out_shape=jax.ShapeDtypeStruct((11, 32, 4096), BF1...  92.5 us
    unnamed x7, local copies, waits for them, and re-layouts  4.69 us

profile of v2, /device:TPU:1, one launch (start us, length us, event | category | flops | bytes accessed | tf_op | source)
XLA Modules:
  0.0 97.9 jit_solution(17284380403956526842)
XLA Ops:
  0.0 0.8 reshape.18.pair_ref
  0.8 0.0 copy-start
  0.8 1.5 %copy-done = bf16[4,4,2,7,4096]{4,2,3,1,0:T(2,128)(2,1)S(1)} copy-done((bf16[4,4,2,7,4096]{4,2,3,1,0:T(2,128)(2,1)S(1)}, bf16[4,4,2,7,4096]{4,2,3,1,0:T(2,128)(2,1)}, u32[]{:S(2)}) %copy-start) | copy-done | bytes 1835032
  2.3 0.0 copy-start.1
  2.3 0.9 copy-done.1
  3.2 0.0 copy-start.2
  3.2 0.7 copy-done.2
  3.9 92.5 %shard_map.46 = bf16[11,32,4096]{2,1,0:T(8,128)(2,1)S(1)} custom-call(s32[8]{0:T(128)S(1)} %reshape.18.pair_ref, s32[16]{0:T(128)S(1)} %bitcast.15, bf16[16,7,64,128]{3,2,1,0:T(8,128)(2,1)S(1)} %bitcast.13, bf16[16,64,128]{2,1,0:T(8,128)(2,1)S(1)} %bitcast.14), custom_call_target="tpu_custom_call" | custom-call | flops 1073741824 | bytes 8388608 | tf_op jit(solution)/shard_map/pallas_call | solution.py:269
  96.3 1.6 %copy.8 = bf16[32,11,4096]{2,0,1:T(8,128)(2,1)} copy(bf16[32,11,4096]{2,0,1:T(8,128)(2,1)S(1)} %bitcast.12) | data formatting | bytes 5767168
Async XLA Ops:
  0.8 1.5 %copy-start = (bf16[4,4,2,7,4096]{4,2,3,1,0:T(2,128)(2,1)S(1)}, bf16[4,4,2,7,4096]{4,2,3,1,0:T(2,128)(2,1)}, u32[]{:S(2)}) copy-start(bf16[4,4,2,7,4096]{4,2,3,1,0:T(2,128)(2,1)} %param.4) | copy-start | bytes 5505028
  2.3 0.9 copy-start.1
  3.2 0.7 copy-start.2

commit v3 on v2

--- a/solution.py
+++ b/solution.py
@@ -1,3 +1,5 @@
+import functools
+
 import jax
 import jax.numpy as jnp
 from jax import lax
@@ -9,6 +11,18 @@
 F32 = jnp.float32
 BF16 = jnp.bfloat16
 GX, GY, GZ = 16, 4, 4
+AXES = (
+    ("gx", GX, lambda: lax.axis_index("gx")),
+    ("gy", GY, lambda: lax.axis_index("gy")),
+    ("gz", GZ, lambda: lax.axis_index("gz")),
+)
+GROUPS = GX // 2
+CASES = (
+    [()]
+    + [(g, g + GROUPS) for g in range(GROUPS)]
+    + [(g, g + GROUPS, h, h + GROUPS) for g in range(GROUPS) for h in range(g + 1, GROUPS)]
+    + [tuple(range(GX))]
+)
 
 
 def iota(shape, dim):
@@ -23,28 +37,25 @@
     return jnp.dot(a, b, preferred_element_type=F32)
 
 
-def kernel(pair_ref, route_ref, a_ref, p_ref, out_ref,
-           nn, nr, ppt, hx, hy, hz, zs, gal, rows, send, recv, anchors,
-           hs_sem, hr_sem, s_sem, r_sem):
+def kernel(pair_ref, route_ref, a_hbm, p_hbm, recv, rows, anchors, choice,
+           a_ref, p_ref, nn, nr, ppt, hx, hy, hz, zs, gal, send, mine, seen_x, seen_y, seen_z,
+           in_sem, hs_sem, hr_sem, s_sem, r_sem, fs_sem, fr_sem):
     gx, gy, gz = lax.axis_index("gx"), lax.axis_index("gy"), lax.axis_index("gz")
 
+    load_p = pltpu.make_async_copy(p_hbm, p_ref, in_sem.at[0])
+    load_a = pltpu.make_async_copy(a_hbm, a_ref, in_sem.at[1])
+    load_p.start()
+    load_a.start()
     barrier = pltpu.get_barrier_semaphore()
-
-    def greet(k, carry):
-        pl.semaphore_signal(barrier, inc=1, device_id={"gx": lax.rem(gx + k, GX)}, device_id_type=MESH)
-        return carry
-
-    lax.fori_loop(1, GX, greet, 0)
+    for name, size, at in AXES:
+        @pl.loop(1, size)
+        def _(k):
+            pl.semaphore_signal(barrier, inc=1, device_id={name: lax.rem(at() + k, size)}, device_id_type=MESH)
     sides = (
         (gx > 0, {"gx": gx - 1}), (gx < GX - 1, {"gx": gx + 1}),
         (gy > 0, {"gy": gy - 1}), (gy < GY - 1, {"gy": gy + 1}),
         (gz > 0, {"gz": gz - 1}), (gz < GZ - 1, {"gz": gz + 1}),
     )
-    for there, device in sides[2:]:
-        @pl.when(there)
-        def _():
-            pl.semaphore_signal(barrier, inc=1, device_id=device, device_id_type=MESH)
-
     left = iota((64, 128), 1) < 64
 
     ci, ki = iota((64, 128), 0), iota((64, 128), 1)
@@ -75,12 +86,46 @@
                 zs[1, i] = jnp.where(left, high, tile).astype(BF16)
         return carry
 
+    load_p.wait()
     lax.fori_loop(0, 8, prepare, 0)
 
-    near = jnp.int32(GX - 1)
-    for there, _ in sides[2:]:
-        near = near + there.astype(jnp.int32)
-    pl.semaphore_wait(barrier, near)
+    lane = iota((8, 128), 1)
+
+    def anchor(d, flags):
+        def look(k, state):
+            one, two = state
+            hit = route_ref[k, 0] == d
+            two = jnp.where(hit & (one < 16) & (two == 16), k, two)
+            one = jnp.where(hit & (one == 16), k, one)
+            return one, two
+
+        one, two = lax.fori_loop(0, 16, look, (jnp.int32(16), jnp.int32(16)))
+        anchors[2 * d] = one
+        anchors[2 * d + 1] = two
+        return jnp.where((lane == d) & (two < 16), 1.0, flags)
+
+    mine[0] = lax.fori_loop(0, GX, anchor, jnp.zeros((8, 128), F32))
+    pl.semaphore_wait(barrier, GX + GY + GZ - 3)
+
+    def tell(stage, k, seen):
+        name, size, at = AXES[stage]
+        return pltpu.make_async_remote_copy(
+            src_ref=mine.at[stage], dst_ref=seen.at[k], send_sem=fs_sem.at[stage, k], recv_sem=fr_sem.at[stage, k],
+            device_id={name: lax.rem(at() + k, size)}, device_id_type=MESH,
+        )
+
+    stages = (seen_x, seen_y, seen_z)
+
+    def tell_all(stage):
+        for k in range(1, AXES[stage][1]):
+            tell(stage, k, stages[stage]).start()
+
+    def hear_all(stage):
+        flags = mine[stage]
+        for k in range(1, AXES[stage][1]):
+            tell(stage, k, stages[stage]).wait()
+            flags = jnp.maximum(flags, stages[stage][k])
+        return flags
 
     faces = (
         (nn.at[0], hx.at[1]), (nn.at[3], hx.at[0]),
@@ -105,6 +150,8 @@
         def _():
             own_halo[i][...] = jnp.zeros(own_halo[i].shape, BF16)
 
+    tell_all(0)
+    load_a.wait()
     zero = jnp.zeros((64, 128), BF16)
     left32 = iota((32, 128), 1) < 64
 
@@ -140,6 +187,9 @@
         for k in range(4):
             product(k * 4 + i + 1, 3, nn[k, i])
             product(k * 4 + i, 4, nn[k, i + 1])
+
+    mine[1] = hear_all(0)
+    tell_all(1)
 
     for i in range(6):
         @pl.when(sides[i][0])
@@ -169,23 +219,13 @@
             product(xy, 5, jnp.where(left, below[u].astype(BF16), own))
             product(xy, 6, jnp.where(left, own, above[u].astype(BF16)))
 
-    @pl.loop(0, GX)
-    def _(d):
-        def look(k, state):
-            one, two = state
-            hit = route_ref[k] == d
-            two = jnp.where(hit & (one < 16) & (two == 16), k, two)
-            one = jnp.where(hit & (one == 16), k, one)
-            return one, two
-
-        one, two = lax.fori_loop(0, 16, look, (jnp.int32(16), jnp.int32(16)))
-        anchors[2 * d] = one
-        anchors[2 * d + 1] = two
+    mine[2] = hear_all(1)
+    tell_all(2)
 
     @pl.loop(0, 16)
     def _(k):
         a, b, z, t = k // 8, (k // 4) % 2, (k // 2) % 2, k % 2
-        along = pair_ref[k // 2] == 0
+        along = pair_ref[a, b, z] == 0
         corner = a * 8 + b * 2
         first = jnp.where(along, corner + t, corner + 4 * t)
         second = jnp.where(along, corner + 4 + t, corner + 4 * t + 1)
@@ -203,11 +243,6 @@
             for j in range(5):
                 rows[k, 1 + 5 * i + j] = block(xy, jnp.where(along, slots_x[i][j], slots_y[i][j])).astype(BF16)
 
-    def pick(d, c):
-        k = anchors[2 * d + c]
-        row = rows[jnp.minimum(k, 15)]
-        return jnp.where(k < 16, row, jnp.zeros_like(row))
-
     def outgoing(k):
         return pltpu.make_async_remote_copy(
             src_ref=send.at[k], dst_ref=recv.at[gx], send_sem=s_sem.at[k], recv_sem=r_sem.at[k],
@@ -216,49 +251,110 @@
 
     @pl.loop(1, GX)
     def _(k):
-        d = lax.rem(gx + k, GX)
-        for c in range(2):
-            send[k, c] = pick(d, c)
+        send[k] = pick(rows, anchors, lax.rem(gx + k, GX), 0)
         outgoing(k).start()
 
-    for c in range(2):
-        recv[gx, c] = pick(gx, c)
+    recv[gx] = pick(rows, anchors, gx, 0)
+
+    flags = hear_all(2)[0:1]
+    flags = jnp.where(iota((1, 128), 1) < GROUPS, jnp.maximum(flags, pltpu.roll(flags, 128 - GROUPS, 1)), 0.0)
+    place = iota((1, 128), 1).astype(F32)
+    count = jnp.sum(flags)
+    high = jnp.max(jnp.where(flags > 0, place, 0.0))
+    low = jnp.min(jnp.where(flags > 0, place, 128.0))
+    two = 1.0 + GROUPS + low * (2 * GROUPS - 1 - low) * 0.5 + (high - low - 1.0)
+    case = jnp.where(count > 2.5, 1.0 * (len(CASES) - 1), jnp.where(count > 1.5, two, jnp.where(count > 0.5, 1.0 + low, 0.0)))
+    choice[0] = case.astype(jnp.int32)
 
     for i in range(6):
         @pl.when(sides[i][0])
         def _():
             halo(i).wait_send()
 
+    @pl.loop(1, GX)
+    def _(k):
+        outgoing(k).wait()
+
+
+def pick(rows, anchors, d, c):
+    k = anchors[2 * d + c]
+    row = rows[jnp.minimum(k, 15)]
+    return jnp.where(k < 16, row, jnp.zeros_like(row))
+
+
+def second(dests, rows, anchors, recv, send, s_sem, r_sem):
+    gx = lax.axis_index("gx")
+    barrier = pltpu.get_barrier_semaphore()
+
+    def copy(i, target, source):
+        return pltpu.make_async_remote_copy(
+            src_ref=send.at[i], dst_ref=recv.at[source], send_sem=s_sem.at[i], recv_sem=r_sem.at[source],
+            device_id={"gx": target}, device_id_type=MESH,
+        )
+
+    hot = functools.reduce(jnp.logical_or, [gx == d for d in dests])
+
+    @pl.when(hot)
+    def _():
+        @pl.loop(1, GX)
+        def _(k):
+            pl.semaphore_signal(barrier, inc=1, device_id={"gx": lax.rem(gx + k, GX)}, device_id_type=MESH)
+
+    for i, d in enumerate(dests):
+        send[i] = pick(rows, anchors, d, 1)
+    pl.semaphore_wait(barrier, len(dests) - hot.astype(jnp.int32))
+    for i, d in enumerate(dests):
+        @pl.when(gx != d)
+        def _():
+            copy(i, d, gx).start()
+
+        @pl.when(gx == d)
+        def _():
+            recv[gx] = send[i]
+
+    @pl.when(jnp.logical_not(hot))
+    def _():
+        @pl.loop(0, GX)
+        def _(s):
+            recv[s] = jnp.zeros(recv.shape[1:], BF16)
+
+    @pl.when(hot)
+    def _():
+        @pl.loop(1, GX)
+        def _(k):
+            s = lax.rem(gx + k, GX)
+            copy(0, s, s).wait_recv()
+
+    for i, d in enumerate(dests):
+        @pl.when(gx != d)
+        def _():
+            copy(i, d, gx).wait_send()
+
+
+def finish(one, two, out_hbm, out, sem):
     pi, qi = iota((256, 256), 0), iota((256, 256), 1)
     turn = ones_where((qi % 32 == pi // 8) & (qi // 32 == pi % 8))
 
-    for g in range(2):
-        @pl.loop(8 * g, 8 * g + 8)
-        def _(s):
-            k = lax.rem(gx - s + GX, GX)
-
-            @pl.when(k != 0)
-            def _():
-                pltpu.make_async_remote_copy(
-                    src_ref=send.at[k], dst_ref=recv.at[s], send_sem=s_sem.at[k], recv_sem=r_sem.at[k],
-                    device_id={"gx": s}, device_id_type=MESH,
-                ).wait_recv()
-
-        @pl.loop(0, 11)
-        def _(b):
+    def store(b):
+        return pltpu.make_async_copy(out.at[b], out_hbm.at[b], sem.at[b])
+
+    @pl.loop(0, 11)
+    def _(b):
+        for g in range(2):
             parts = []
             for h in range(2):
                 x = jnp.concatenate(
-                    [recv[8 * g + 4 * h + s, c, b] for s in range(4) for c in range(2)], axis=0
+                    [ref[8 * g + 4 * h + s, b] for s in range(4) for ref in (one, two)], axis=0
                 )
                 parts.append(dot(turn, x).reshape(32, 8, 128))
             tile = jnp.concatenate(parts, axis=1).astype(BF16)
             for j in range(32):
-                out_ref[b, pl.ds(16 * g, 16), pl.ds(128 * j, 128)] = tile[j]
-
-    @pl.loop(1, GX)
-    def _(k):
-        outgoing(k).wait_send()
+                out[b, pl.ds(16 * g, 16), pl.ds(128 * j, 128)] = tile[j]
+        store(b).start()
+
+    @pl.loop(0, 11)
+    def _(b):
+        store(b).wait()
 
 
 def local(a_blocks, prolong, pairing, route):
@@ -266,12 +362,16 @@
     p = prolong.reshape(4, 4, 2, 32, 128).transpose(0, 1, 3, 2, 4).reshape(16, 64, 128)
     smem = pl.BlockSpec(memory_space=pltpu.SMEM)
     vmem = pl.BlockSpec(memory_space=pltpu.VMEM)
-    out = pl.pallas_call(
+    hbm = pl.BlockSpec(memory_space=pltpu.HBM)
+    row_set = jax.ShapeDtypeStruct((16, 11, 32, 128), BF16)
+    one, rows, anchors, choice = pl.pallas_call(
         kernel,
-        out_shape=jax.ShapeDtypeStruct((11, 32, 4096), BF16),
-        in_specs=[smem, smem, vmem, vmem],
-        out_specs=vmem,
+        out_shape=(row_set, row_set, jax.ShapeDtypeStruct((32,), jnp.int32), jax.ShapeDtypeStruct((1,), jnp.int32)),
+        in_specs=[smem, smem, hbm, hbm],
+        out_specs=(vmem, vmem, smem, smem),
         scratch_shapes=[
+            pltpu.VMEM((16, 7, 64, 128), BF16),
+            pltpu.VMEM((16, 64, 128), BF16),
             pltpu.VMEM((4, 4, 64, 128), BF16),
             pltpu.VMEM((16, 64, 128), BF16),
             pltpu.VMEM((16, 128, 128), BF16),
@@ -281,19 +381,55 @@
             pltpu.VMEM((2, 8, 64, 128), BF16),
             pltpu.VMEM((224, 32, 128), F32),
             pltpu.VMEM((16, 11, 32, 128), BF16),
-            pltpu.VMEM((16, 2, 11, 32, 128), BF16),
-            pltpu.VMEM((16, 2, 11, 32, 128), BF16),
-            pltpu.SMEM((32,), jnp.int32),
+            pltpu.VMEM((3, 8, 128), F32),
+            pltpu.VMEM((GX, 8, 128), F32),
+            pltpu.VMEM((GY, 8, 128), F32),
+            pltpu.VMEM((GZ, 8, 128), F32),
+            pltpu.SemaphoreType.DMA((2,)),
             pltpu.SemaphoreType.DMA((6,)),
             pltpu.SemaphoreType.DMA((6,)),
             pltpu.SemaphoreType.DMA((16,)),
             pltpu.SemaphoreType.DMA((16,)),
+            pltpu.SemaphoreType.DMA((3, 16)),
+            pltpu.SemaphoreType.DMA((3, 16)),
         ],
         compiler_params=pltpu.CompilerParams(
-            collective_id=0, has_side_effects=True, vmem_limit_bytes=48 << 20
+            collective_id=0, has_side_effects=True, vmem_limit_bytes=40 << 20
         ),
         cost_estimate=pl.CostEstimate(flops=1 << 30, bytes_accessed=8 << 20, transcendentals=0),
-    )(pairing.reshape(8), route.reshape(16), a, p)
+    )(pairing, route, a, p)
+
+    def exchange(number):
+        dests = CASES[number]
+        if not dests:
+            return lambda rows, anchors: jnp.zeros(row_set.shape, BF16)
+        return pl.pallas_call(
+            functools.partial(second, dests),
+            out_shape=row_set,
+            in_specs=[vmem, smem],
+            out_specs=vmem,
+            scratch_shapes=[
+                pltpu.VMEM((len(dests), 11, 32, 128), BF16),
+                pltpu.SemaphoreType.DMA((len(dests),)),
+                pltpu.SemaphoreType.DMA((GX,)),
+            ],
+            compiler_params=pltpu.CompilerParams(
+                collective_id=number, has_side_effects=True, vmem_limit_bytes=40 << 20
+            ),
+            cost_estimate=pl.CostEstimate(flops=0, bytes_accessed=4 << 20, transcendentals=0),
+        )
+
+    two = lax.switch(choice[0], [exchange(i) for i in range(len(CASES))], rows, anchors)
+
+    out = pl.pallas_call(
+        finish,
+        out_shape=jax.ShapeDtypeStruct((11, 32, 4096), BF16),
+        in_specs=[vmem, vmem],
+        out_specs=hbm,
+        scratch_shapes=[pltpu.VMEM((11, 32, 4096), BF16), pltpu.SemaphoreType.DMA((11,))],
+        compiler_params=pltpu.CompilerParams(vmem_limit_bytes=40 << 20),
+        cost_estimate=pl.CostEstimate(flops=1 << 30, bytes_accessed=6 << 20, transcendentals=0),
+    )(one, two)
     return out.transpose(1, 0, 2)
 
 

time: 98.1 us -> 84.6 us (0.86)
  the two profiles are of different devices: /device:TPU:1 before, /device:TPU:124 now
where the time goes in v3:
time: 84.6 us; the launch traced here: 84.4 us
  Pallas kernels  79.3 us (94%)
  local copies, waits for them, and re-layouts  3.86 us (5%)
    pallas_call x1, Pallas kernels, local(): pl.pallas_call(kernel, out_shape=(row_set, row_set, jax.ShapeDtypeStruct(...  53.3 us
    pallas_call x1, Pallas kernels, local(): lax.switch(choice[0], [exchange(i) for i in range(len(CASES))], rows, anc...  20.6 us
    pallas_call x1, Pallas kernels, local(): pl.pallas_call(finish, out_shape=jax.ShapeDtypeStruct((11, 32, 4096), BF1...  5.39 us
    unnamed x7, local copies, waits for them, and re-layouts  3.86 us

profile of v3, /device:TPU:124, one launch (start us, length us, event | category | flops | bytes accessed | tf_op | source)
XLA Modules:
  0.0 84.4 jit_solution(8020128208061014326)
XLA Ops:
  0.0 0.7 copy.7.route_ref
  0.7 0.0 copy-start
  0.7 1.5 %copy-done = bf16[4,4,2,7,4096]{4,2,3,1,0:T(2,128)(2,1)S(1)} copy-done((bf16[4,4,2,7,4096]{4,2,3,1,0:T(2,128)(2,1)S(1)}, bf16[4,4,2,7,4096]{4,2,3,1,0:T(2,128)(2,1)}, u32[]{:S(2)}) %copy-start) | copy-done | bytes 1835032
  2.2 0.0 copy-start.1
  2.2 0.9 %copy-done.1 = bf16[4,4,2,4096]{3,2,1,0:T(2,128)(2,1)S(1)} copy-done((bf16[4,4,2,4096]{3,2,1,0:T(2,128)(2,1)S(1)}, bf16[4,4,2,4096]{3,2,1,0:T(2,128)(2,1)}, u32[]{:S(2)}) %copy-start.1) | copy-done | bytes 262168
  3.2 0.0 copy-start.2
  3.2 0.7 copy-done.2
  3.9 53.3 %shard_map.46 = (bf16[16,11,32,128]{3,2,1,0:T(8,128)(2,1)S(1)}, bf16[16,11,32,128]{3,2,1,0:T(8,128)(2,1)S(1)}, s32[32]{0:T(128)S(1)}, s32[1]{0:T(128)}) custom-call(s32[2,2,2]{2,1,0:T(2,128)S(1)} %copy-done.2, s32[16,1]{1,0:T(8,128)S(1)} %copy.7.route_ref, bf16[16,7,64,128]{3,2,1,0:T(8,128)(2,1)S(1)} %bitcast.12, bf16[16,64,128]{2,1,0:T(8,128)(2,1)S(1)} %bitcast.13), custom_call_target="tpu_custom_call" | custom-call | flops 1073741824 | bytes 8388608 | tf_op jit(solution)/shard_map/pallas_call | solution.py:367
  57.8 21.1 %conditional.1 = (bf16[16,11,32,128]{3,2,1,0:T(8,128)(2,1)}) conditional(s32[]{:T(128)} %bitcast.6, () %tuple.119, (bf16[16,11,32,128]{3,2,1,0:T(8,128)(2,1)S(1)}, s32[32]{0:T(128)S(1)}) %tuple.120, (bf16[16,11,32,128]{3,2,1,0:T(8,128)(2,1)S(1)}, s32[32]{0:T(128)S(1)}) %tuple.120, ...), branch_computations={%region_0.0_spmd, %region_1.0_spmd, %region_2.0_spmd, %region_3.0_... | conditional | bytes 4194312 | solution.py:422
  58.0 20.6 %branch_29_fun.1 = bf16[16,11,32,128]{3,2,1,0:T(8,128)(2,1)} custom-call(bf16[16,11,32,128]{3,2,1,0:T(8,128)(2,1)S(1)} %get-tuple-element.248.rows, s32[32]{0:T(128)S(1)} %get-tuple-element.249.anchors), custom_call_target="tpu_custom_call" | custom-call | bytes 4194304 | tf_op jit(solution)/shard_map/cond/branch_29_fun/pallas_call | solution.py:422
  78.9 5.4 %shard_map.47 = bf16[11,32,4096]{2,1,0:T(8,128)(2,1)} custom-call(bf16[16,11,32,128]{3,2,1,0:T(8,128)(2,1)S(1)} %get-tuple-element.270.one, bf16[16,11,32,128]{3,2,1,0:T(8,128)(2,1)} %get-tuple-element.274.two), custom_call_target="tpu_custom_call" | custom-call | flops 1073741824 | bytes 6291456 | tf_op jit(solution)/shard_map/pallas_call | solution.py:424
Async XLA Ops:
  0.7 1.5 %copy-start = (bf16[4,4,2,7,4096]{4,2,3,1,0:T(2,128)(2,1)S(1)}, bf16[4,4,2,7,4096]{4,2,3,1,0:T(2,128)(2,1)}, u32[]{:S(2)}) copy-start(bf16[4,4,2,7,4096]{4,2,3,1,0:T(2,128)(2,1)} %param.42) | copy-start | bytes 5505028
  2.2 0.9 %copy-start.1 = (bf16[4,4,2,4096]{3,2,1,0:T(2,128)(2,1)S(1)}, bf16[4,4,2,4096]{3,2,1,0:T(2,128)(2,1)}, u32[]{:S(2)}) copy-start(bf16[4,4,2,4096]{3,2,1,0:T(2,128)(2,1)} %param.43) | copy-start | bytes 786436
  3.2 0.7 copy-start.2

commit v4 on v3

--- a/solution.py
+++ b/solution.py
@@ -37,14 +37,18 @@
     return jnp.dot(a, b, preferred_element_type=F32)
 
 
-def kernel(pair_ref, route_ref, a_hbm, p_hbm, recv, rows, anchors, choice,
-           a_ref, p_ref, nn, nr, ppt, hx, hy, hz, zs, gal, send, mine, seen_x, seen_y, seen_z,
+def kernel(pair_hbm, route_hbm, a_hbm, p_hbm, recv, others, choice,
+           pair_ref, route_ref, a_ref, p_ref, rows, anchors, nn, nr, ppt, hx, hy, hz, zs, gal, send, mine, seen_x, seen_y, seen_z,
            in_sem, hs_sem, hr_sem, s_sem, r_sem, fs_sem, fr_sem):
     gx, gy, gz = lax.axis_index("gx"), lax.axis_index("gy"), lax.axis_index("gz")
 
     load_p = pltpu.make_async_copy(p_hbm, p_ref, in_sem.at[0])
     load_a = pltpu.make_async_copy(a_hbm, a_ref, in_sem.at[1])
+    load_route = pltpu.make_async_copy(route_hbm, route_ref, in_sem.at[2])
+    load_pair = pltpu.make_async_copy(pair_hbm, pair_ref, in_sem.at[3])
     load_p.start()
+    load_route.start()
+    load_pair.start()
     load_a.start()
     barrier = pltpu.get_barrier_semaphore()
     for name, size, at in AXES:
@@ -94,7 +98,7 @@
     def anchor(d, flags):
         def look(k, state):
             one, two = state
-            hit = route_ref[k, 0] == d
+            hit = route_ref[k] == d
             two = jnp.where(hit & (one < 16) & (two == 16), k, two)
             one = jnp.where(hit & (one == 16), k, one)
             return one, two
@@ -104,6 +108,7 @@
         anchors[2 * d + 1] = two
         return jnp.where((lane == d) & (two < 16), 1.0, flags)
 
+    load_route.wait()
     mine[0] = lax.fori_loop(0, GX, anchor, jnp.zeros((8, 128), F32))
     pl.semaphore_wait(barrier, GX + GY + GZ - 3)
 
@@ -152,6 +157,7 @@
 
     tell_all(0)
     load_a.wait()
+    load_pair.wait()
     zero = jnp.zeros((64, 128), BF16)
     left32 = iota((32, 128), 1) < 64
 
@@ -256,8 +262,13 @@
 
     recv[gx] = pick(rows, anchors, gx, 0)
 
+    @pl.loop(0, GX)
+    def _(d):
+        others[d] = pick(rows, anchors, d, 1)
+
     flags = hear_all(2)[0:1]
-    flags = jnp.where(iota((1, 128), 1) < GROUPS, jnp.maximum(flags, pltpu.roll(flags, 128 - GROUPS, 1)), 0.0)
+    flags = jnp.maximum(flags, pltpu.roll(flags, 128 - GROUPS, 1))
+    flags = jnp.where(iota((1, 128), 1) < GROUPS, flags, 0.0)
     place = iota((1, 128), 1).astype(F32)
     count = jnp.sum(flags)
     high = jnp.max(jnp.where(flags > 0, place, 0.0))
@@ -265,6 +276,7 @@
     two = 1.0 + GROUPS + low * (2 * GROUPS - 1 - low) * 0.5 + (high - low - 1.0)
     case = jnp.where(count > 2.5, 1.0 * (len(CASES) - 1), jnp.where(count > 1.5, two, jnp.where(count > 0.5, 1.0 + low, 0.0)))
     choice[0] = case.astype(jnp.int32)
+    choice[1] = (jnp.sum(jnp.where(place == lax.rem(gx, GROUPS).astype(F32), flags, 0.0)) > 0.5).astype(jnp.int32)
 
     for i in range(6):
         @pl.when(sides[i][0])
@@ -282,17 +294,11 @@
     return jnp.where(k < 16, row, jnp.zeros_like(row))
 
 
-def second(dests, rows, anchors, recv, send, s_sem, r_sem):
+def second(dests, rows, recv, s_sem, r_sem):
     gx = lax.axis_index("gx")
     barrier = pltpu.get_barrier_semaphore()
-
-    def copy(i, target, source):
-        return pltpu.make_async_remote_copy(
-            src_ref=send.at[i], dst_ref=recv.at[source], send_sem=s_sem.at[i], recv_sem=r_sem.at[source],
-            device_id={"gx": target}, device_id_type=MESH,
-        )
-
-    hot = functools.reduce(jnp.logical_or, [gx == d for d in dests])
+    number = len(dests)
+    hot = functools.reduce(jnp.logical_or, [gx == d for d in dests]) if number < GX else gx >= 0
 
     @pl.when(hot)
     def _():
@@ -300,38 +306,41 @@
         def _(k):
             pl.semaphore_signal(barrier, inc=1, device_id={"gx": lax.rem(gx + k, GX)}, device_id_type=MESH)
 
-    for i, d in enumerate(dests):
-        send[i] = pick(rows, anchors, d, 1)
-    pl.semaphore_wait(barrier, len(dests) - hot.astype(jnp.int32))
-    for i, d in enumerate(dests):
+    def copy(source, target, device):
+        return pltpu.make_async_remote_copy(
+            src_ref=source, dst_ref=target, send_sem=s_sem, recv_sem=r_sem,
+            device_id={"gx": device}, device_id_type=MESH,
+        )
+
+    def bytes_of(n):
+        return copy(rows.at[pl.ds(0, n)], recv.at[pl.ds(0, n)], 0)
+
+    pl.semaphore_wait(barrier, number - hot.astype(jnp.int32))
+
+    @pl.loop(0, number)
+    def _(i):
+        if number == GX:
+            d = lax.rem(gx + i, GX)
+        else:
+            d = dests[0] + GROUPS * lax.rem(i, 2)
+            d = jnp.where(i < 2, d, d + dests[-2] - dests[0])
+
         @pl.when(gx != d)
         def _():
-            copy(i, d, gx).start()
-
-        @pl.when(gx == d)
-        def _():
-            recv[gx] = send[i]
+            copy(rows.at[d], recv.at[gx], d).start()
+
+    @pl.when(hot)
+    def _():
+        bytes_of(GX - 1).wait_recv()
+        bytes_of(number - 1).wait_send()
 
     @pl.when(jnp.logical_not(hot))
     def _():
-        @pl.loop(0, GX)
-        def _(s):
-            recv[s] = jnp.zeros(recv.shape[1:], BF16)
-
-    @pl.when(hot)
-    def _():
-        @pl.loop(1, GX)
-        def _(k):
-            s = lax.rem(gx + k, GX)
-            copy(0, s, s).wait_recv()
-
-    for i, d in enumerate(dests):
-        @pl.when(gx != d)
-        def _():
-            copy(i, d, gx).wait_send()
-
-
-def finish(one, two, out_hbm, out, sem):
+        bytes_of(number).wait_send()
+
+
+def finish(choice, one, two, own, out_hbm, out, sem):
+    hot, gx = choice[1] == 1, lax.axis_index("gx")
     pi, qi = iota((256, 256), 0), iota((256, 256), 1)
     turn = ones_where((qi % 32 == pi // 8) & (qi // 32 == pi % 8))
 
@@ -343,9 +352,11 @@
         for g in range(2):
             parts = []
             for h in range(2):
-                x = jnp.concatenate(
-                    [ref[8 * g + 4 * h + s, b] for s in range(4) for ref in (one, two)], axis=0
-                )
+                x = []
+                for s in range(8 * g + 4 * h, 8 * g + 4 * h + 4):
+                    late = jnp.where(gx == s, own[gx, b], two[s, b])
+                    x += [one[s, b], jnp.where(hot, late, jnp.zeros_like(late))]
+                x = jnp.concatenate(x, axis=0)
                 parts.append(dot(turn, x).reshape(32, 8, 128))
             tile = jnp.concatenate(parts, axis=1).astype(BF16)
             for j in range(32):
@@ -364,14 +375,18 @@
     vmem = pl.BlockSpec(memory_space=pltpu.VMEM)
     hbm = pl.BlockSpec(memory_space=pltpu.HBM)
     row_set = jax.ShapeDtypeStruct((16, 11, 32, 128), BF16)
-    one, rows, anchors, choice = pl.pallas_call(
+    one, others, choice = pl.pallas_call(
         kernel,
-        out_shape=(row_set, row_set, jax.ShapeDtypeStruct((32,), jnp.int32), jax.ShapeDtypeStruct((1,), jnp.int32)),
-        in_specs=[smem, smem, hbm, hbm],
-        out_specs=(vmem, vmem, smem, smem),
+        out_shape=(row_set, row_set, jax.ShapeDtypeStruct((2,), jnp.int32)),
+        in_specs=[hbm, hbm, hbm, hbm],
+        out_specs=(vmem, vmem, smem),
         scratch_shapes=[
+            pltpu.SMEM((2, 2, 2), jnp.int32),
+            pltpu.SMEM((16,), jnp.int32),
             pltpu.VMEM((16, 7, 64, 128), BF16),
             pltpu.VMEM((16, 64, 128), BF16),
+            pltpu.VMEM((16, 11, 32, 128), BF16),
+            pltpu.SMEM((32,), jnp.int32),
             pltpu.VMEM((4, 4, 64, 128), BF16),
             pltpu.VMEM((16, 64, 128), BF16),
             pltpu.VMEM((16, 128, 128), BF16),
@@ -385,7 +400,7 @@
             pltpu.VMEM((GX, 8, 128), F32),
             pltpu.VMEM((GY, 8, 128), F32),
             pltpu.VMEM((GZ, 8, 128), F32),
-            pltpu.SemaphoreType.DMA((2,)),
+            pltpu.SemaphoreType.DMA((4,)),
             pltpu.SemaphoreType.DMA((6,)),
             pltpu.SemaphoreType.DMA((6,)),
             pltpu.SemaphoreType.DMA((16,)),
@@ -394,24 +409,23 @@
             pltpu.SemaphoreType.DMA((3, 16)),
         ],
         compiler_params=pltpu.CompilerParams(
-            collective_id=0, has_side_effects=True, vmem_limit_bytes=40 << 20
+            collective_id=0, has_side_effects=True, vmem_limit_bytes=60 << 20
         ),
         cost_estimate=pl.CostEstimate(flops=1 << 30, bytes_accessed=8 << 20, transcendentals=0),
-    )(pairing, route, a, p)
+    )(pairing, route.reshape(16), a, p)
 
     def exchange(number):
         dests = CASES[number]
         if not dests:
-            return lambda rows, anchors: jnp.zeros(row_set.shape, BF16)
+            return lambda rows: rows
         return pl.pallas_call(
             functools.partial(second, dests),
             out_shape=row_set,
-            in_specs=[vmem, smem],
+            in_specs=[vmem],
             out_specs=vmem,
             scratch_shapes=[
-                pltpu.VMEM((len(dests), 11, 32, 128), BF16),
-                pltpu.SemaphoreType.DMA((len(dests),)),
-                pltpu.SemaphoreType.DMA((GX,)),
+                pltpu.SemaphoreType.DMA,
+                pltpu.SemaphoreType.DMA,
             ],
             compiler_params=pltpu.CompilerParams(
                 collective_id=number, has_side_effects=True, vmem_limit_bytes=40 << 20
@@ -419,17 +433,17 @@
             cost_estimate=pl.CostEstimate(flops=0, bytes_accessed=4 << 20, transcendentals=0),
         )
 
-    two = lax.switch(choice[0], [exchange(i) for i in range(len(CASES))], rows, anchors)
+    two = lax.switch(choice[0], [exchange(i) for i in range(len(CASES))], others)
 
     out = pl.pallas_call(
         finish,
         out_shape=jax.ShapeDtypeStruct((11, 32, 4096), BF16),
-        in_specs=[vmem, vmem],
+        in_specs=[smem, vmem, vmem, vmem],
         out_specs=hbm,
         scratch_shapes=[pltpu.VMEM((11, 32, 4096), BF16), pltpu.SemaphoreType.DMA((11,))],
         compiler_params=pltpu.CompilerParams(vmem_limit_bytes=40 << 20),
         cost_estimate=pl.CostEstimate(flops=1 << 30, bytes_accessed=6 << 20, transcendentals=0),
-    )(one, two)
+    )(choice, one, two, others)
     return out.transpose(1, 0, 2)
 
 

time: 84.6 us -> 79.7 us (0.942)
  the two profiles are of different devices: /device:TPU:124 before, /device:TPU:46 now
where the time goes in v4:
time: 79.7 us; the launch traced here: 79.6 us
  Pallas kernels  78.9 us (99%)
    pallas_call x1, Pallas kernels, local(): pl.pallas_call(kernel, out_shape=(row_set, row_set, jax.ShapeDtypeStruct(...  55.4 us
    pallas_call x1, Pallas kernels, local(): lax.switch(choice[0], [exchange(i) for i in range(len(CASES))], others)  17.8 us
    pallas_call x1, Pallas kernels, local(): pl.pallas_call(finish, out_shape=jax.ShapeDtypeStruct((11, 32, 4096), BF1...  5.61 us

profile of v4, /device:TPU:46, one launch (start us, length us, event | category | flops | bytes accessed | tf_op | source)
XLA Modules:
  0.0 79.6 jit_solution(9544809320121587715)
XLA Ops:
  0.0 55.4 %shard_map.46 = (bf16[16,11,32,128]{3,2,1,0:T(8,128)(2,1)}, bf16[16,11,32,128]{3,2,1,0:T(8,128)(2,1)S(1)}, s32[2]{0:T(128)}) custom-call(s32[2,2,2]{2,1,0:T(2,128)} %pair_hbm.1, s32[16]{0:T(128)} %bitcast.17, bf16[16,7,64,128]{3,2,1,0:T(8,128)(2,1)} %bitcast.15, bf16[16,64,128]{2,1,0:T(8,128)(2,1)} %bitcast.16), custom_call_target="tpu_custom_call" | custom-call | flops 1073741824 | bytes 8388608 | tf_op jit(solution)/shard_map/pallas_call | solution.py:378
  56.0 0.0 copy-start
  56.0 0.0 copy-start.1
  56.0 17.9 %conditional.1 = (bf16[16,11,32,128]{3,2,1,0:T(8,128)(2,1)}) conditional(s32[]{:T(128)} %bitcast.7, bf16[16,11,32,128]{3,2,1,0:T(8,128)(2,1)S(1)} %get-tuple-element.87.own, bf16[16,11,32,128]{3,2,1,0:T(8,128)(2,1)S(1)} %get-tuple-element.87.own, bf16[16,11,32,128]{3,2,1,0:T(8,128)(2,1)S(1)} %get-tuple-element.87.own, ...), branch_computations={%region_0.0_spmd, %region_1.0_spmd, %region_2.0_spmd, %region_3.0_... | conditional | bytes 4194312 | solution.py:436
  56.1 17.8 %branch_26_fun.1 = bf16[16,11,32,128]{3,2,1,0:T(8,128)(2,1)} custom-call(bf16[16,11,32,128]{3,2,1,0:T(8,128)(2,1)S(1)} %rows.25), custom_call_target="tpu_custom_call" | custom-call | bytes 4194304 | tf_op jit(solution)/shard_map/cond/branch_26_fun/pallas_call | solution.py:436
  74.0 0.0 copy-done
  74.0 0.0 copy-done.1
  74.0 5.6 %shard_map.47 = bf16[11,32,4096]{2,1,0:T(8,128)(2,1)} custom-call(s32[2]{0:T(128)S(1)} %copy-done.1, bf16[16,11,32,128]{3,2,1,0:T(8,128)(2,1)S(1)} %copy-done, bf16[16,11,32,128]{3,2,1,0:T(8,128)(2,1)} %get-tuple-element.88.two, bf16[16,11,32,128]{3,2,1,0:T(8,128)(2,1)S(1)} %get-tuple-element.87.own), custom_call_target="tpu_custom_call" | custom-call | flops 1073741824 | bytes 6291456 | tf_op jit(solution)/shard_map/pallas_call | solution.py:438
Async XLA Ops:
  56.0 17.9 %copy-start = (bf16[16,11,32,128]{3,2,1,0:T(8,128)(2,1)S(1)}, bf16[16,11,32,128]{3,2,1,0:T(8,128)(2,1)}, u32[]{:S(2)}) copy-start(bf16[16,11,32,128]{3,2,1,0:T(8,128)(2,1)} %get-tuple-element.86.one) | copy-start | bytes 4325380
  56.0 17.9 %copy-start.1 = (s32[2]{0:T(128)S(1)}, s32[2]{0:T(128)}, u32[]{:S(2)}) copy-start(s32[2]{0:T(128)} %get-tuple-element.85.choice) | copy-start | bytes 28

commit v5 on v4

--- a/solution.py
+++ b/solution.py
@@ -93,6 +93,51 @@
     load_p.wait()
     lax.fori_loop(0, 8, prepare, 0)
 
+    pl.semaphore_wait(barrier, GX + GY + GZ - 3)
+
+    def tell(stage, k, seen):
+        name, size, at = AXES[stage]
+        return pltpu.make_async_remote_copy(
+            src_ref=mine.at[stage], dst_ref=seen.at[k], send_sem=fs_sem.at[stage, k], recv_sem=fr_sem.at[stage, k],
+            device_id={name: lax.rem(at() + k, size)}, device_id_type=MESH,
+        )
+
+    stages = (seen_x, seen_y, seen_z)
+
+    def tell_all(stage):
+        for k in range(1, AXES[stage][1]):
+            tell(stage, k, stages[stage]).start()
+
+    def hear_all(stage):
+        flags = mine[stage]
+        for k in range(1, AXES[stage][1]):
+            tell(stage, k, stages[stage]).wait()
+            flags = jnp.maximum(flags, stages[stage][k])
+        return flags
+
+    faces = (
+        (nn.at[0], hx.at[1]), (nn.at[3], hx.at[0]),
+        (nn.at[:, 0], hy.at[1]), (nn.at[:, 3], hy.at[0]),
+        (zs.at[0], hz.at[1]), (zs.at[1], hz.at[0]),
+    )
+    own_halo = (hx.at[0], hx.at[1], hy.at[0], hy.at[1], hz.at[0], hz.at[1])
+
+    def halo(i):
+        source, target = faces[i]
+        return pltpu.make_async_remote_copy(
+            src_ref=source, dst_ref=target, send_sem=hs_sem.at[i], recv_sem=hr_sem.at[i],
+            device_id=sides[i][1], device_id_type=MESH,
+        )
+
+    for i in (4, 5, 0, 1, 2, 3):
+        @pl.when(sides[i][0])
+        def _():
+            halo(i).start()
+
+        @pl.when(jnp.logical_not(sides[i][0]))
+        def _():
+            own_halo[i][...] = jnp.zeros(own_halo[i].shape, BF16)
+
     lane = iota((8, 128), 1)
 
     def anchor(d, flags):
@@ -103,79 +148,37 @@
             one = jnp.where(hit & (one == 16), k, one)
             return one, two
 
-        one, two = lax.fori_loop(0, 16, look, (jnp.int32(16), jnp.int32(16)))
+        one, two = lax.fori_loop(0, 16, look, (jnp.int32(16), jnp.int32(16)), unroll=True)
         anchors[2 * d] = one
         anchors[2 * d + 1] = two
         return jnp.where((lane == d) & (two < 16), 1.0, flags)
 
     load_route.wait()
     mine[0] = lax.fori_loop(0, GX, anchor, jnp.zeros((8, 128), F32))
-    pl.semaphore_wait(barrier, GX + GY + GZ - 3)
-
-    def tell(stage, k, seen):
-        name, size, at = AXES[stage]
-        return pltpu.make_async_remote_copy(
-            src_ref=mine.at[stage], dst_ref=seen.at[k], send_sem=fs_sem.at[stage, k], recv_sem=fr_sem.at[stage, k],
-            device_id={name: lax.rem(at() + k, size)}, device_id_type=MESH,
-        )
-
-    stages = (seen_x, seen_y, seen_z)
-
-    def tell_all(stage):
-        for k in range(1, AXES[stage][1]):
-            tell(stage, k, stages[stage]).start()
-
-    def hear_all(stage):
-        flags = mine[stage]
-        for k in range(1, AXES[stage][1]):
-            tell(stage, k, stages[stage]).wait()
-            flags = jnp.maximum(flags, stages[stage][k])
-        return flags
-
-    faces = (
-        (nn.at[0], hx.at[1]), (nn.at[3], hx.at[0]),
-        (nn.at[:, 0], hy.at[1]), (nn.at[:, 3], hy.at[0]),
-        (zs.at[0], hz.at[1]), (zs.at[1], hz.at[0]),
-    )
-    own_halo = (hx.at[0], hx.at[1], hy.at[0], hy.at[1], hz.at[0], hz.at[1])
-
-    def halo(i):
-        source, target = faces[i]
-        return pltpu.make_async_remote_copy(
-            src_ref=source, dst_ref=target, send_sem=hs_sem.at[i], recv_sem=hr_sem.at[i],
-            device_id=sides[i][1], device_id_type=MESH,
-        )
-
-    for i in range(6):
-        @pl.when(sides[i][0])
-        def _():
-            halo(i).start()
-
-        @pl.when(jnp.logical_not(sides[i][0]))
-        def _():
-            own_halo[i][...] = jnp.zeros(own_halo[i].shape, BF16)
-
     tell_all(0)
     load_a.wait()
     load_pair.wait()
     zero = jnp.zeros((64, 128), BF16)
     left32 = iota((32, 128), 1) < 64
 
-    def product(xy, s, near_tile):
+    def mix(xy, s, near_tile):
         wide = jnp.concatenate(
             [jnp.concatenate([near_tile, zero], axis=1), jnp.concatenate([zero, near_tile], axis=1)], axis=0
         )
         mixed = dot(a_ref[xy, s], wide).astype(BF16)
-        mixed = jnp.concatenate([mixed[:, :128], mixed[:, 128:]], axis=0)
-        g = dot(ppt[xy], mixed)
+        return jnp.concatenate([mixed[:, :128], mixed[:, 128:]], axis=0)
+
+    def keep(xy, s, g):
         gal[xy * 14 + 2 * s] = jnp.where(left32, g[0:32], pltpu.roll(g[32:64], 64, 1))
         gal[xy * 14 + 2 * s + 1] = jnp.where(left32, pltpu.roll(g[64:96], 64, 1), g[96:128])
 
-    def loop(n, body):
-        def step(i, carry):
-            body(i)
-            return carry
-        lax.fori_loop(0, n, step, 0)
+    def product(xy, s, near_tile):
+        keep(xy, s, dot(ppt[xy], mix(xy, s, near_tile)))
+
+    def products(xy, s, t, near_s, near_t):
+        g = dot(ppt[xy], jnp.concatenate([mix(xy, s, near_s), mix(xy, t, near_t)], axis=1))
+        keep(xy, s, g[:, :128])
+        keep(xy, t, g[:, 128:])
 
     @pl.loop(0, 4)
     def _(x):
@@ -188,16 +191,7 @@
             product(i * 4 + 4 + k, 1, nn[i, k])
             product(i * 4 + k, 2, nn[i + 1, k])
 
-    @pl.loop(0, 3)
-    def _(i):
-        for k in range(4):
-            product(k * 4 + i + 1, 3, nn[k, i])
-            product(k * 4 + i, 4, nn[k, i + 1])
-
-    mine[1] = hear_all(0)
-    tell_all(1)
-
-    for i in range(6):
+    def arrived(i):
         @pl.when(sides[i][0])
         def _():
             j = i ^ 1
@@ -207,12 +201,8 @@
                 device_id=sides[i][1], device_id_type=MESH,
             ).wait_recv()
 
-    @pl.loop(0, 4)
-    def _(k):
-        product(k, 1, hx[0, k])
-        product(12 + k, 2, hx[1, k])
-        product(k * 4, 3, hy[0, k])
-        product(k * 4 + 3, 4, hy[1, k])
+    arrived(4)
+    arrived(5)
 
     @pl.loop(0, 8)
     def _(q):
@@ -222,44 +212,75 @@
         for u in range(2):
             xy = 2 * q + u
             own = nr[xy]
-            product(xy, 5, jnp.where(left, below[u].astype(BF16), own))
-            product(xy, 6, jnp.where(left, own, above[u].astype(BF16)))
-
-    mine[2] = hear_all(1)
-    tell_all(2)
-
-    @pl.loop(0, 16)
-    def _(k):
+            products(xy, 5, 6, jnp.where(left, below[u].astype(BF16), own), jnp.where(left, own, above[u].astype(BF16)))
+
+    def place_of(k):
         a, b, z, t = k // 8, (k // 4) % 2, (k // 2) % 2, k % 2
         along = pair_ref[a, b, z] == 0
         corner = a * 8 + b * 2
         first = jnp.where(along, corner + t, corner + 4 * t)
         second = jnp.where(along, corner + 4 + t, corner + 4 * t + 1)
-
-        def block(xy, s):
-            return gal[xy * 14 + 2 * s + z]
-
-        rows[k, 0] = (
+        return along, first, second, lambda xy, s: gal[xy * 14 + 2 * s + z]
+
+    @pl.loop(0, 16)
+    def _(k):
+        along, first, second, block = place_of(k)
+        for i, xy in enumerate((first, second)):
+            for j in range(2):
+                rows[k, 2 * i + j] = block(xy, 5 + j).astype(BF16)
+
+    parts = (pl.ds(0, 4), pl.ds(4, 7))
+
+    def outgoing(part, k):
+        return pltpu.make_async_remote_copy(
+            src_ref=send.at[k, parts[part]], dst_ref=recv.at[gx, parts[part]],
+            send_sem=s_sem.at[part, k], recv_sem=r_sem.at[part, k],
+            device_id={"gx": lax.rem(gx + k, GX)}, device_id_type=MESH,
+        )
+
+    def post(part):
+        @pl.loop(1, GX)
+        def _(k):
+            send[k, parts[part]] = pick(rows, anchors, lax.rem(gx + k, GX), 0, parts[part])
+            outgoing(part, k).start()
+
+    post(0)
+
+    @pl.loop(0, 3)
+    def _(i):
+        for k in range(4):
+            product(k * 4 + i + 1, 3, nn[k, i])
+            product(k * 4 + i, 4, nn[k, i + 1])
+
+    mine[1] = hear_all(0)
+    tell_all(1)
+    for i in range(4):
+        arrived(i)
+
+    @pl.loop(0, 4)
+    def _(k):
+        product(k, 1, hx[0, k])
+        product(12 + k, 2, hx[1, k])
+        product(k * 4, 3, hy[0, k])
+        product(k * 4 + 3, 4, hy[1, k])
+
+    mine[2] = hear_all(1)
+    tell_all(2)
+
+    @pl.loop(0, 16)
+    def _(k):
+        along, first, second, block = place_of(k)
+        rows[k, 4] = (
             block(first, 0) + block(second, 0)
             + block(first, jnp.where(along, 2, 4)) + block(second, jnp.where(along, 1, 3))
         ).astype(BF16)
-        slots_x = ((1, 3, 4, 5, 6), (2, 3, 4, 5, 6))
-        slots_y = ((1, 2, 3, 5, 6), (1, 2, 4, 5, 6))
+        slots_x = ((1, 3, 4), (2, 3, 4))
+        slots_y = ((1, 2, 3), (1, 2, 4))
         for i, xy in enumerate((first, second)):
-            for j in range(5):
-                rows[k, 1 + 5 * i + j] = block(xy, jnp.where(along, slots_x[i][j], slots_y[i][j])).astype(BF16)
-
-    def outgoing(k):
-        return pltpu.make_async_remote_copy(
-            src_ref=send.at[k], dst_ref=recv.at[gx], send_sem=s_sem.at[k], recv_sem=r_sem.at[k],
-            device_id={"gx": lax.rem(gx + k, GX)}, device_id_type=MESH,
-        )
-
-    @pl.loop(1, GX)
-    def _(k):
-        send[k] = pick(rows, anchors, lax.rem(gx + k, GX), 0)
-        outgoing(k).start()
-
+            for j in range(3):
+                rows[k, 5 + 3 * i + j] = block(xy, jnp.where(along, slots_x[i][j], slots_y[i][j])).astype(BF16)
+
+    post(1)
     recv[gx] = pick(rows, anchors, gx, 0)
 
     @pl.loop(0, GX)
@@ -285,16 +306,17 @@
 
     @pl.loop(1, GX)
     def _(k):
-        outgoing(k).wait()
-
-
-def pick(rows, anchors, d, c):
+        outgoing(0, k).wait()
+        outgoing(1, k).wait()
+
+
+def pick(rows, anchors, d, c, part=slice(None)):
     k = anchors[2 * d + c]
-    row = rows[jnp.minimum(k, 15)]
+    row = rows[jnp.minimum(k, 15), part]
     return jnp.where(k < 16, row, jnp.zeros_like(row))
 
 
-def second(dests, rows, recv, s_sem, r_sem):
+def second(dests, rows, recv, s_sem, r_sem, own_sem):
     gx = lax.axis_index("gx")
     barrier = pltpu.get_barrier_semaphore()
     number = len(dests)
@@ -331,6 +353,9 @@
 
     @pl.when(hot)
     def _():
+        own = pltpu.make_async_copy(rows.at[gx], recv.at[gx], own_sem)
+        own.start()
+        own.wait()
         bytes_of(GX - 1).wait_recv()
         bytes_of(number - 1).wait_send()
 
@@ -339,29 +364,34 @@
         bytes_of(number).wait_send()
 
 
-def finish(choice, one, two, own, out_hbm, out, sem):
-    hot, gx = choice[1] == 1, lax.axis_index("gx")
+def finish(choice, one, two, out_hbm, out, sem):
     pi, qi = iota((256, 256), 0), iota((256, 256), 1)
     turn = ones_where((qi % 32 == pi // 8) & (qi // 32 == pi % 8))
+    zero = jnp.zeros((32, 128), BF16)
 
     def store(b):
         return pltpu.make_async_copy(out.at[b], out_hbm.at[b], sem.at[b])
 
-    @pl.loop(0, 11)
-    def _(b):
-        for g in range(2):
-            parts = []
-            for h in range(2):
-                x = []
-                for s in range(8 * g + 4 * h, 8 * g + 4 * h + 4):
-                    late = jnp.where(gx == s, own[gx, b], two[s, b])
-                    x += [one[s, b], jnp.where(hot, late, jnp.zeros_like(late))]
-                x = jnp.concatenate(x, axis=0)
-                parts.append(dot(turn, x).reshape(32, 8, 128))
-            tile = jnp.concatenate(parts, axis=1).astype(BF16)
-            for j in range(32):
-                out[b, pl.ds(16 * g, 16), pl.ds(128 * j, 128)] = tile[j]
-        store(b).start()
+    def turned(hot):
+        @pl.loop(0, 11)
+        def _(i):
+            b = jnp.where(i < 4, 4 + i % 2 + 5 * (i // 2), jnp.where(i < 8, i - 4, i - 2))
+            for g in range(2):
+                x = [
+                    jnp.concatenate(
+                        [t for s in range(4) for t in (one[8 * g + 4 * h + s, i], two[8 * g + 4 * h + s, i] if hot else zero)],
+                        axis=0,
+                    )
+                    for h in range(2)
+                ]
+                y = dot(turn, jnp.concatenate(x, axis=1))
+                tile = jnp.concatenate([y[:, :128].reshape(32, 8, 128), y[:, 128:].reshape(32, 8, 128)], axis=1).astype(BF16)
+                for j in range(32):
+                    out[b, pl.ds(16 * g, 16), pl.ds(128 * j, 128)] = tile[j]
+            store(b).start()
+
+    pl.when(choice[1] == 1)(lambda: turned(True))
+    pl.when(choice[1] != 1)(lambda: turned(False))
 
     @pl.loop(0, 11)
     def _(b):
@@ -403,8 +433,8 @@
             pltpu.SemaphoreType.DMA((4,)),
             pltpu.SemaphoreType.DMA((6,)),
             pltpu.SemaphoreType.DMA((6,)),
-            pltpu.SemaphoreType.DMA((16,)),
-            pltpu.SemaphoreType.DMA((16,)),
+            pltpu.SemaphoreType.DMA((2, 16)),
+            pltpu.SemaphoreType.DMA((2, 16)),
             pltpu.SemaphoreType.DMA((3, 16)),
             pltpu.SemaphoreType.DMA((3, 16)),
         ],
@@ -426,6 +456,7 @@
             scratch_shapes=[
                 pltpu.SemaphoreType.DMA,
                 pltpu.SemaphoreType.DMA,
+                pltpu.SemaphoreType.DMA,
             ],
             compiler_params=pltpu.CompilerParams(
                 collective_id=number, has_side_effects=True, vmem_limit_bytes=40 << 20
@@ -438,12 +469,12 @@
     out = pl.pallas_call(
         finish,
         out_shape=jax.ShapeDtypeStruct((11, 32, 4096), BF16),
-        in_specs=[smem, vmem, vmem, vmem],
+        in_specs=[smem, vmem, vmem],
         out_specs=hbm,
         scratch_shapes=[pltpu.VMEM((11, 32, 4096), BF16), pltpu.SemaphoreType.DMA((11,))],
         compiler_params=pltpu.CompilerParams(vmem_limit_bytes=40 << 20),
         cost_estimate=pl.CostEstimate(flops=1 << 30, bytes_accessed=6 << 20, transcendentals=0),
-    )(choice, one, two, others)
+    )(choice, one, two)
     return out.transpose(1, 0, 2)
 
 

time: 79.7 us -> 68.1 us (0.85)
  the two profiles are of different devices: /device:TPU:46 before, /device:TPU:1 now
where the time goes in v5:
time: 68.1 us; the launch traced here: 68 us
  Pallas kernels  66.6 us (98%)
  between operations  0.85 us (1%)
    pallas_call x1, Pallas kernels, local(): pl.pallas_call(kernel, out_shape=(row_set, row_set, jax.ShapeDtypeStruct(...  53.1 us
    pallas_call x1, Pallas kernels, local(): lax.switch(choice[0], [exchange(i) for i in range(len(CASES))], others)  9.65 us
    pallas_call x1, Pallas kernels, local(): pl.pallas_call(finish, out_shape=jax.ShapeDtypeStruct((11, 32, 4096), BF1...  3.89 us

profile of v5, /device:TPU:1, one launch (start us, length us, event | category | flops | bytes accessed | tf_op | source)
XLA Modules:
  0.0 68.0 jit_solution(3100901473752295602)
XLA Ops:
  0.0 53.1 %shard_map.46 = (bf16[16,11,32,128]{3,2,1,0:T(8,128)(2,1)}, bf16[16,11,32,128]{3,2,1,0:T(8,128)(2,1)S(1)}, s32[2]{0:T(128)}) custom-call(s32[2,2,2]{2,1,0:T(2,128)} %pair_hbm.1, s32[16]{0:T(128)} %bitcast.17, bf16[16,7,64,128]{3,2,1,0:T(8,128)(2,1)} %bitcast.15, bf16[16,64,128]{2,1,0:T(8,128)(2,1)} %bitcast.16), custom_call_target="tpu_custom_call" | custom-call | flops 1073741824 | bytes 8388608 | tf_op jit(solution)/shard_map/pallas_call | solution.py:408
  53.7 0.0 copy-start
  53.7 0.0 copy-start.1
  53.7 10.2 %conditional.1 = (bf16[16,11,32,128]{3,2,1,0:T(8,128)(2,1)S(1)}) conditional(s32[]{:T(128)} %bitcast.7, bf16[16,11,32,128]{3,2,1,0:T(8,128)(2,1)S(1)} %get-tuple-element.87, bf16[16,11,32,128]{3,2,1,0:T(8,128)(2,1)S(1)} %get-tuple-element.87, bf16[16,11,32,128]{3,2,1,0:T(8,128)(2,1)S(1)} %get-tuple-element.87, ...), branch_computations={%region_0.0_spmd, %region_1.0_spmd, %region_2.0_spmd, %region_3.0_... | conditional | bytes 7077896 | solution.py:467
  53.8 0.2 copy.88.rows
  54.0 9.7 %branch_7_fun.1 = bf16[16,11,32,128]{3,2,1,0:T(8,128)(2,1)S(1)} custom-call(bf16[16,11,32,128]{3,2,1,0:T(8,128)(2,1)S(1)} %copy.88.rows), custom_call_target="tpu_custom_call" | custom-call | bytes 4194304 | tf_op jit(solution)/shard_map/cond/branch_7_fun/pallas_call | solution.py:467
  63.9 0.0 copy-done
  63.9 0.0 copy-done.1
  63.9 3.9 %shard_map.47 = bf16[11,32,4096]{2,1,0:T(8,128)(2,1)} custom-call(s32[2]{0:T(128)S(1)} %copy-done.1, bf16[16,11,32,128]{3,2,1,0:T(8,128)(2,1)S(1)} %copy-done, bf16[16,11,32,128]{3,2,1,0:T(8,128)(2,1)S(1)} %get-tuple-element.88.two), custom_call_target="tpu_custom_call" | custom-call | flops 1073741824 | bytes 6291456 | tf_op jit(solution)/shard_map/pallas_call | solution.py:469
Async XLA Ops:
  53.7 10.2 %copy-start = (bf16[16,11,32,128]{3,2,1,0:T(8,128)(2,1)S(1)}, bf16[16,11,32,128]{3,2,1,0:T(8,128)(2,1)}, u32[]{:S(2)}) copy-start(bf16[16,11,32,128]{3,2,1,0:T(8,128)(2,1)} %get-tuple-element.86.one) | copy-start | bytes 4325380
  53.7 10.2 %copy-start.1 = (s32[2]{0:T(128)S(1)}, s32[2]{0:T(128)}, u32[]{:S(2)}) copy-start(s32[2]{0:T(128)} %get-tuple-element.85.choice) | copy-start | bytes 28

commit v6 on v5

--- a/solution.py
+++ b/solution.py
@@ -18,10 +18,9 @@
 )
 GROUPS = GX // 2
 CASES = (
-    [()]
-    + [(g, g + GROUPS) for g in range(GROUPS)]
+    [tuple(range(GX))]
+    + [(g, g + GROUPS) for g in range(0, GROUPS, 2)]
     + [(g, g + GROUPS, h, h + GROUPS) for g in range(GROUPS) for h in range(g + 1, GROUPS)]
-    + [tuple(range(GX))]
 )
 
 
@@ -70,28 +69,23 @@
     z_lane = (ri % 2) == (li // 64)
     half_row = (ri // 64) == (li // 64)
 
-    def prepare(i, carry):
-        for u in range(2):
-            xy = 2 * i + u
-            raw = p_ref[xy].astype(F32)
+    load_p.wait()
+
+    @pl.loop(0, 4)
+    def _(x):
+        tiles = []
+        for y in range(4):
+            raw = p_ref[4 * x + y].astype(F32)
             both = jnp.concatenate([raw, pltpu.roll(raw, 64, 1)], axis=0)
             tile = dot(order, jnp.where(z_lane, both, 0.0).astype(BF16))
-            nn[xy // 4, xy % 4] = tile.astype(BF16)
             turned = pltpu.roll(tile, 64, 1)
-            nr[xy] = turned.astype(BF16)
-            twice = jnp.concatenate([raw, raw], axis=0)
-            twice = jnp.where(half_row, twice, 0.0).astype(BF16)
-            t = lax.dot_general(spread, twice, (((1,), (1,)), ((), ())), preferred_element_type=F32)
-            ppt[xy] = jnp.where(same_z, t, 0.0).astype(BF16)
-            if u == 0:
-                low, high = tile, turned
-            else:
-                zs[0, i] = jnp.where(left, low, turned).astype(BF16)
-                zs[1, i] = jnp.where(left, high, tile).astype(BF16)
-        return carry
-
-    load_p.wait()
-    lax.fori_loop(0, 8, prepare, 0)
+            nn[x, y] = tile.astype(BF16)
+            nr[4 * x + y] = turned.astype(BF16)
+            tiles.append((tile, turned))
+        for h in range(2):
+            (low, high), (tile, turned) = tiles[2 * h], tiles[2 * h + 1]
+            zs[0, 2 * x + h] = jnp.where(left, low, turned).astype(BF16)
+            zs[1, 2 * x + h] = jnp.where(left, high, tile).astype(BF16)
 
     pl.semaphore_wait(barrier, GX + GY + GZ - 3)
 
@@ -137,6 +131,14 @@
         @pl.when(jnp.logical_not(sides[i][0]))
         def _():
             own_halo[i][...] = jnp.zeros(own_halo[i].shape, BF16)
+
+    @pl.loop(0, 4)
+    def _(x):
+        for y in range(4):
+            raw = p_ref[4 * x + y].astype(F32)
+            twice = jnp.where(half_row, jnp.concatenate([raw, raw], axis=0), 0.0).astype(BF16)
+            t = lax.dot_general(spread, twice, (((1,), (1,)), ((), ())), preferred_element_type=F32)
+            ppt[4 * x + y] = jnp.where(same_z, t, 0.0).astype(BF16)
 
     lane = iota((8, 128), 1)
 
@@ -180,10 +182,11 @@
         keep(xy, s, g[:, :128])
         keep(xy, t, g[:, 128:])
 
-    @pl.loop(0, 4)
-    def _(x):
-        for y in range(4):
-            product(x * 4 + y, 0, nn[x, y])
+    @pl.loop(0, 2)
+    def _(h):
+        for u in range(2):
+            for y in range(4):
+                product(8 * h + 4 * u + y, 0, nn[2 * h + u, y])
 
     @pl.loop(0, 3)
     def _(i):
@@ -204,15 +207,16 @@
     arrived(4)
     arrived(5)
 
-    @pl.loop(0, 8)
-    def _(q):
-        below, above = hz[0, q].astype(F32), hz[1, q].astype(F32)
-        below = (below, pltpu.roll(below, 64, 1))
-        above = (pltpu.roll(above, 64, 1), above)
-        for u in range(2):
-            xy = 2 * q + u
-            own = nr[xy]
-            products(xy, 5, 6, jnp.where(left, below[u].astype(BF16), own), jnp.where(left, own, above[u].astype(BF16)))
+    @pl.loop(0, 4)
+    def _(x):
+        for q in range(2):
+            below, above = hz[0, 2 * x + q].astype(F32), hz[1, 2 * x + q].astype(F32)
+            below = (below, pltpu.roll(below, 64, 1))
+            above = (pltpu.roll(above, 64, 1), above)
+            for u in range(2):
+                xy = 4 * x + 2 * q + u
+                own = nr[xy]
+                products(xy, 5, 6, jnp.where(left, below[u].astype(BF16), own), jnp.where(left, own, above[u].astype(BF16)))
 
     def place_of(k):
         a, b, z, t = k // 8, (k // 4) % 2, (k // 2) % 2, k % 2
@@ -293,9 +297,14 @@
     place = iota((1, 128), 1).astype(F32)
     count = jnp.sum(flags)
     high = jnp.max(jnp.where(flags > 0, place, 0.0))
-    low = jnp.min(jnp.where(flags > 0, place, 128.0))
-    two = 1.0 + GROUPS + low * (2 * GROUPS - 1 - low) * 0.5 + (high - low - 1.0)
-    case = jnp.where(count > 2.5, 1.0 * (len(CASES) - 1), jnp.where(count > 1.5, two, jnp.where(count > 0.5, 1.0 + low, 0.0)))
+    low = jnp.where(count > 0.5, jnp.min(jnp.where(flags > 0, place, 128.0)), 0.0)
+    alone, half = count < 1.5, GROUPS // 2
+    odd = low - 2.0 * jnp.floor(low * 0.5) > 0.5
+    even_case = 1.0 + low * 0.5
+    low = jnp.where(alone & (low >= half), low - half, low)
+    high = jnp.where(alone, low + half, high)
+    two = 1.0 + half + low * (2 * GROUPS - 1 - low) * 0.5 + (high - low - 1.0)
+    case = jnp.where(count > 2.5, 0.0, jnp.where(alone & jnp.logical_not(odd), even_case, two))
     choice[0] = case.astype(jnp.int32)
     choice[1] = (jnp.sum(jnp.where(place == lax.rem(gx, GROUPS).astype(F32), flags, 0.0)) > 0.5).astype(jnp.int32)
 
@@ -446,8 +455,6 @@
 
     def exchange(number):
         dests = CASES[number]
-        if not dests:
-            return lambda rows: rows
         return pl.pallas_call(
             functools.partial(second, dests),
             out_shape=row_set,
@@ -459,7 +466,7 @@
                 pltpu.SemaphoreType.DMA,
             ],
             compiler_params=pltpu.CompilerParams(
-                collective_id=number, has_side_effects=True, vmem_limit_bytes=40 << 20
+                collective_id=1 + number, has_side_effects=True, vmem_limit_bytes=40 << 20
             ),
             cost_estimate=pl.CostEstimate(flops=0, bytes_accessed=4 << 20, transcendentals=0),
         )

time: 68.1 us -> 74.3 us (1.091)
  Pallas kernels: 66.6 us -> 73.5 us
    pallas_call x1, Pallas kernels: 9.65 us -> 17.3 us  [local(): lax.switch(choice[0], [exchange(i) for i in range(len(CASES))], others)]
    pallas_call x1, Pallas kernels: 53.1 us -> 51.4 us  [local(): pl.pallas_call(kernel, out_shape=(row_set, row_set, jax.ShapeDtypeStruct(...]
    pallas_call x1, Pallas kernels: 3.89 us -> 4.81 us  [local(): pl.pallas_call(finish, out_shape=jax.ShapeDtypeStruct((11, 32, 4096), BF1...]
where the time goes in v6:
time: 74.3 us; the launch traced here: 74.2 us
  Pallas kernels  73.5 us (99%)
    pallas_call x1, Pallas kernels, local(): pl.pallas_call(kernel, out_shape=(row_set, row_set, jax.ShapeDtypeStruct(...  51.4 us
    pallas_call x1, Pallas kernels, local(): lax.switch(choice[0], [exchange(i) for i in range(len(CASES))], others)  17.3 us
    pallas_call x1, Pallas kernels, local(): pl.pallas_call(finish, out_shape=jax.ShapeDtypeStruct((11, 32, 4096), BF1...  4.81 us

profile of v6, /device:TPU:1, one launch (start us, length us, event | category | flops | bytes accessed | tf_op | source)
XLA Modules:
  0.0 74.2 jit_solution(10092173126554007109)
XLA Ops:
  0.0 51.4 %shard_map.46 = (bf16[16,11,32,128]{3,2,1,0:T(8,128)(2,1)}, bf16[16,11,32,128]{3,2,1,0:T(8,128)(2,1)S(1)}, s32[2]{0:T(128)}) custom-call(s32[2,2,2]{2,1,0:T(2,128)} %pair_hbm.1, s32[16]{0:T(128)} %bitcast.17, bf16[16,7,64,128]{3,2,1,0:T(8,128)(2,1)} %bitcast.15, bf16[16,64,128]{2,1,0:T(8,128)(2,1)} %bitcast.16), custom_call_target="tpu_custom_call" | custom-call | flops 1073741824 | bytes 8388608 | tf_op jit(solution)/shard_map/pallas_call | solution.py:417
  52.0 0.0 copy-start
  52.0 0.0 copy-start.1
  52.0 17.3 %conditional.1 = (bf16[16,11,32,128]{3,2,1,0:T(8,128)(2,1)}) conditional(s32[]{:T(128)} %bitcast.7, bf16[16,11,32,128]{3,2,1,0:T(8,128)(2,1)S(1)} %get-tuple-element.77, bf16[16,11,32,128]{3,2,1,0:T(8,128)(2,1)S(1)} %get-tuple-element.77, bf16[16,11,32,128]{3,2,1,0:T(8,128)(2,1)S(1)} %get-tuple-element.77, ...), branch_computations={%region_0.0_spmd, %region_1.0_spmd, %region_2.0_spmd, %region_3.0_... | conditional | bytes 4194312 | solution.py:474
  52.1 17.3 %branch_14_fun.1 = bf16[16,11,32,128]{3,2,1,0:T(8,128)(2,1)} custom-call(bf16[16,11,32,128]{3,2,1,0:T(8,128)(2,1)S(1)} %rows.14), custom_call_target="tpu_custom_call" | custom-call | bytes 4194304 | tf_op jit(solution)/shard_map/cond/branch_14_fun/pallas_call | solution.py:474
  69.3 0.0 copy-done
  69.4 0.0 copy-done.1
  69.4 4.8 %shard_map.47 = bf16[11,32,4096]{2,1,0:T(8,128)(2,1)} custom-call(s32[2]{0:T(128)S(1)} %copy-done.1, bf16[16,11,32,128]{3,2,1,0:T(8,128)(2,1)S(1)} %copy-done, bf16[16,11,32,128]{3,2,1,0:T(8,128)(2,1)} %get-tuple-element.78.two), custom_call_target="tpu_custom_call" | custom-call | flops 1073741824 | bytes 6291456 | tf_op jit(solution)/shard_map/pallas_call | solution.py:476
Async XLA Ops:
  52.0 17.4 %copy-start = (bf16[16,11,32,128]{3,2,1,0:T(8,128)(2,1)S(1)}, bf16[16,11,32,128]{3,2,1,0:T(8,128)(2,1)}, u32[]{:S(2)}) copy-start(bf16[16,11,32,128]{3,2,1,0:T(8,128)(2,1)} %get-tuple-element.76.one) | copy-start | bytes 4325380
  52.0 17.4 %copy-start.1 = (s32[2]{0:T(128)S(1)}, s32[2]{0:T(128)}, u32[]{:S(2)}) copy-start(s32[2]{0:T(128)} %get-tuple-element.75.choice) | copy-start | bytes 28

commit v7 on v6

--- a/solution.py
+++ b/solution.py
@@ -346,6 +346,9 @@
     def bytes_of(n):
         return copy(rows.at[pl.ds(0, n)], recv.at[pl.ds(0, n)], 0)
 
+    away = lax.rem(gx // 2 - dests[0] // 2 + GROUPS, GROUPS)
+    tie = (away == 2) | (away == 6)
+    far = (((away > 2) & (away < 6)) | (tie & (gx % 2 == 1))).astype(jnp.int32)
     pl.semaphore_wait(barrier, number - hot.astype(jnp.int32))
 
     @pl.loop(0, number)
@@ -353,7 +356,7 @@
         if number == GX:
             d = lax.rem(gx + i, GX)
         else:
-            d = dests[0] + GROUPS * lax.rem(i, 2)
+            d = dests[0] + GROUPS * lax.rem(i + far, 2)
             d = jnp.where(i < 2, d, d + dests[-2] - dests[0])
 
         @pl.when(gx != d)
@@ -364,8 +367,8 @@
     def _():
         own = pltpu.make_async_copy(rows.at[gx], recv.at[gx], own_sem)
         own.start()
+        bytes_of(GX - 1).wait_recv()
         own.wait()
-        bytes_of(GX - 1).wait_recv()
         bytes_of(number - 1).wait_send()
 
     @pl.when(jnp.logical_not(hot))

time: 74.3 us -> 73.9 us (level)
  Pallas kernels: 73.5 us -> 72.5 us
    pallas_call x1, Pallas kernels: 17.3 us -> 16.3 us  [local(): lax.switch(choice[0], [exchange(i) for i in range(len(CASES))], others)]
where the time goes in v7:
time: 73.9 us; the launch traced here: 73.2 us
  Pallas kernels  72.5 us (98%)
    pallas_call x1, Pallas kernels, local(): pl.pallas_call(kernel, out_shape=(row_set, row_set, jax.ShapeDtypeStruct(...  51.4 us
    pallas_call x1, Pallas kernels, local(): lax.switch(choice[0], [exchange(i) for i in range(len(CASES))], others)  16.3 us
    pallas_call x1, Pallas kernels, local(): pl.pallas_call(finish, out_shape=jax.ShapeDtypeStruct((11, 32, 4096), BF1...  4.72 us

profile of v7, /device:TPU:1, one launch (start us, length us, event | category | flops | bytes accessed | tf_op | source)
XLA Modules:
  0.0 73.2 jit_solution(12960164427986185715)
XLA Ops:
  0.0 51.4 %shard_map.46 = (bf16[16,11,32,128]{3,2,1,0:T(8,128)(2,1)}, bf16[16,11,32,128]{3,2,1,0:T(8,128)(2,1)S(1)}, s32[2]{0:T(128)}) custom-call(s32[2,2,2]{2,1,0:T(2,128)} %pair_hbm.1, s32[16]{0:T(128)} %bitcast.17, bf16[16,7,64,128]{3,2,1,0:T(8,128)(2,1)} %bitcast.15, bf16[16,64,128]{2,1,0:T(8,128)(2,1)} %bitcast.16), custom_call_target="tpu_custom_call" | custom-call | flops 1073741824 | bytes 8388608 | tf_op jit(solution)/shard_map/pallas_call | solution.py:420
  52.0 0.0 copy-start
  52.0 0.0 copy-start.1
  52.0 16.4 %conditional.1 = (bf16[16,11,32,128]{3,2,1,0:T(8,128)(2,1)}) conditional(s32[]{:T(128)} %bitcast.7, bf16[16,11,32,128]{3,2,1,0:T(8,128)(2,1)S(1)} %get-tuple-element.77, bf16[16,11,32,128]{3,2,1,0:T(8,128)(2,1)S(1)} %get-tuple-element.77, bf16[16,11,32,128]{3,2,1,0:T(8,128)(2,1)S(1)} %get-tuple-element.77, ...), branch_computations={%region_0.0_spmd, %region_1.0_spmd, %region_2.0_spmd, %region_3.0_... | conditional | bytes 4194312 | solution.py:477
  52.1 16.3 %branch_23_fun.1 = bf16[16,11,32,128]{3,2,1,0:T(8,128)(2,1)} custom-call(bf16[16,11,32,128]{3,2,1,0:T(8,128)(2,1)S(1)} %rows.23), custom_call_target="tpu_custom_call" | custom-call | bytes 4194304 | tf_op jit(solution)/shard_map/cond/branch_23_fun/pallas_call | solution.py:477
  68.4 0.0 copy-done
  68.4 0.0 copy-done.1
  68.5 4.7 %shard_map.47 = bf16[11,32,4096]{2,1,0:T(8,128)(2,1)} custom-call(s32[2]{0:T(128)S(1)} %copy-done.1, bf16[16,11,32,128]{3,2,1,0:T(8,128)(2,1)S(1)} %copy-done, bf16[16,11,32,128]{3,2,1,0:T(8,128)(2,1)} %get-tuple-element.78.two), custom_call_target="tpu_custom_call" | custom-call | flops 1073741824 | bytes 6291456 | tf_op jit(solution)/shard_map/pallas_call | solution.py:479
Async XLA Ops:
  52.0 16.4 %copy-start = (bf16[16,11,32,128]{3,2,1,0:T(8,128)(2,1)S(1)}, bf16[16,11,32,128]{3,2,1,0:T(8,128)(2,1)}, u32[]{:S(2)}) copy-start(bf16[16,11,32,128]{3,2,1,0:T(8,128)(2,1)} %get-tuple-element.76.one) | copy-start | bytes 4325380
  52.0 16.4 %copy-start.1 = (s32[2]{0:T(128)S(1)}, s32[2]{0:T(128)}, u32[]{:S(2)}) copy-start(s32[2]{0:T(128)} %get-tuple-element.75.choice) | copy-start | bytes 28
